TPU v7x, 128 devices: a whole 4x4x4 slice. The times are simulated.
128 devices in a mesh: grp: 2 (over x_hi), prompt: 8 (over y, core), resp: 8 (over z, x_lo).
Axes of the slice: x: 4 (x_hi: 2, x_lo: 2; x = x_hi * 2 + x_lo), y: 4, z: 4, core: 2. Of those that a mesh axis runs over, the one named last changes fastest.
Arguments:
- prompt_states: bfloat16 [2, 512, 4096], P('grp', 'prompt'), may hold values from -6 to 6
- response_states: bfloat16 [2, 64, 512, 4096], P('grp', ('prompt', 'resp')), may hold values from -6 to 6
- queries: bfloat16 [2, 64, 512, 2048], P('grp', ('prompt', 'resp'))
- grad_output: bfloat16 [2, 64, 512, 2048], P('grp', ('prompt', 'resp')), may hold values from -24 to 24
- key_weight: bfloat16 [4096, 512], replicated, may hold values from -0.09375 to 0.09375
- value_weight: bfloat16 [4096, 512], replicated, may hold values from -0.09375 to 0.09375
- rewards: float32 [2, 64], P('grp', ('prompt', 'resp'))
- lengths: int32 [2, 64], P('grp', ('prompt', 'resp')), may hold values from 1 to 512, 19660 in all within a row
- group_ids: int32 [2, 64], P('grp', ('prompt', 'resp')), may hold values from 0 to 7
Outputs:
- query_grad: bfloat16 [2, 64, 512, 2048], P('grp', ('prompt', 'resp'))
- key_weight_grad: float32 [4096, 512], P(('prompt', 'resp'))
- value_weight_grad: float32 [4096, 512], P(('prompt', 'resp'))
Inputs may be any that keep to these rules, and one draw needn't show every extreme that they name: `lengths`: token slots at and above a response's length are padding; in every rollout group some response has all 512.
All inputs are finite; a program needn't handle non-finite values.
Results may differ from a plain program's by a relative error of at most 0.009.
The roundings to bfloat16 on the way count: a program that leaves them out, or rounds other values in their place, can miss the bound.
Values may be sent and summed in bfloat16 or wider, within the bound.
A program may use at most 128 MiB of HBM per device.

v0:
```python
import jax
import jax.numpy as jnp
from jax import lax
from jax.sharding import PartitionSpec as P

HEAD_DIM = 128
RLEN = 512
QBLOCK = 128
NADV = 8


THETA = 1000000.0
EPS = 1e-06


def rotary_tables(positions, half):
    steps = jnp.arange(half, dtype=jnp.float32)
    freq = THETA ** (-2.0 * steps / (2.0 * half))
    angle = positions.astype(jnp.float32)[:, None] * freq[None, :]
    return (jnp.cos(angle)[:, None, :], jnp.sin(angle)[:, None, :])


def finish_keys(raw, positions):
    count = raw.shape[0]
    heads = raw.reshape(count, -1, HEAD_DIM)
    factor = lax.rsqrt(jnp.mean(heads * heads, axis=-1, keepdims=True) + EPS)
    normed = heads * factor
    half = HEAD_DIM // 2
    cosine, sine = rotary_tables(positions, half)
    first = normed[..., :half]
    second = normed[..., half:]
    turned = jnp.concatenate(
        [first * cosine - second * sine, second * cosine + first * sine], axis=-1
    )
    return turned.reshape(count, -1)


def keys_backward(grad, raw, positions):
    count = raw.shape[0]
    heads = raw.reshape(count, -1, HEAD_DIM)
    factor = lax.rsqrt(jnp.mean(heads * heads, axis=-1, keepdims=True) + EPS)
    normed = heads * factor
    half = HEAD_DIM // 2
    cosine, sine = rotary_tables(positions, half)
    upper = grad.reshape(count, -1, HEAD_DIM)
    grad_a = upper[..., :half]
    grad_b = upper[..., half:]
    unturned = jnp.concatenate(
        [grad_a * cosine + grad_b * sine, grad_b * cosine - grad_a * sine], axis=-1
    )
    inner = jnp.mean(unturned * normed, axis=-1, keepdims=True)
    return (factor * (unturned - normed * inner)).reshape(count, -1)


def attend(query, dout, keys, values, row_start, prompt_len):
    rows = query.shape[0]
    total = keys.shape[0]
    kv_heads = keys.shape[1] // HEAD_DIM
    fold = query.shape[1] // keys.shape[1]
    scale = HEAD_DIM ** (-0.5)
    q_all = query.reshape(rows, kv_heads, fold, HEAD_DIM)
    k_all = keys.reshape(total, kv_heads, HEAD_DIM)
    v_all = values.reshape(total, kv_heads, HEAD_DIM)
    d_all = dout.reshape(rows, kv_heads, fold, HEAD_DIM)
    scores = jnp.einsum("rhgd,nhd->hgrn", q_all, k_all, preferred_element_type=jnp.float32) * scale
    key_pos = jnp.arange(total, dtype=jnp.int32)
    row_pos = row_start + jnp.arange(rows, dtype=jnp.int32)
    visible = (key_pos[None, :] < prompt_len) | (key_pos[None, :] - prompt_len <= row_pos[:, None])
    scores = jnp.where(visible, scores, -jnp.inf)
    peak = jnp.max(scores, axis=-1, keepdims=True)
    expo = jnp.exp(scores - peak)
    probs = expo / jnp.sum(expo, axis=-1, keepdims=True)
    probs_b = probs.astype(jnp.bfloat16)
    attn = jnp.einsum("hgrn,nhd->rhgd", probs_b, v_all, preferred_element_type=jnp.float32)
    delta = jnp.sum(d_all.astype(jnp.float32) * attn, axis=-1)
    dprobs = jnp.einsum("rhgd,nhd->hgrn", d_all, v_all, preferred_element_type=jnp.float32)
    dscores = (probs * (dprobs - jnp.transpose(delta, (1, 2, 0))[..., None])).astype(jnp.bfloat16)
    grad_q = (
        jnp.einsum("hgrn,nhd->rhgd", dscores, k_all, preferred_element_type=jnp.float32) * scale
    )
    grad_k = (
        jnp.einsum("hgrn,rhgd->nhd", dscores, q_all, preferred_element_type=jnp.float32) * scale
    )
    grad_v = jnp.einsum("hgrn,rhgd->nhd", probs_b, d_all, preferred_element_type=jnp.float32)
    return (
        grad_q.reshape(rows, -1).astype(jnp.bfloat16),
        grad_k.reshape(total, -1),
        grad_v.reshape(total, -1),
    )


def from_sums(rewards, onehot, count, total, square):
    members = jnp.maximum(count, 1.0)
    mean = total / members
    spread = jnp.sqrt(jnp.maximum(square / members - mean * mean, 0.0))
    own_mean = jnp.sum(onehot * mean[None, :], axis=1)
    own_spread = jnp.sum(onehot * spread[None, :], axis=1)
    return (rewards - own_mean) / jnp.maximum(own_spread, 0.5)


def body(
    prompt_states,
    response_states,
    queries,
    grad_output,
    key_weight,
    value_weight,
    rewards,
    lengths,
    group_ids,
):
    width = key_weight.shape[1]
    shard_rows = prompt_states.shape[1]
    local_rewards = rewards[0]
    local_lengths = lengths[0]
    onehot = (group_ids[0][:, None] == jnp.arange(NADV, dtype=jnp.int32)[None, :]).astype(
        jnp.float32
    )
    count = jnp.sum(onehot, axis=0)
    total = jnp.sum(onehot * local_rewards[:, None], axis=0)
    square = jnp.sum(onehot * (local_rewards * local_rewards)[:, None], axis=0)
    sums = lax.psum((count, total, square), ("prompt", "resp"))
    advantage = from_sums(local_rewards, onehot, sums[0], sums[1], sums[2])
    sub_rows = shard_rows // lax.axis_size("resp")
    sub_offset = lax.axis_index("resp") * sub_rows
    slice_positions = (
        lax.axis_index("prompt") * shard_rows + sub_offset + jnp.arange(sub_rows, dtype=jnp.int32)
    )
    slice_rows = lax.dynamic_slice_in_dim(prompt_states[0], sub_offset, sub_rows, 0)
    slice_raw = jnp.dot(slice_rows, key_weight, preferred_element_type=jnp.float32)
    slice_keys = finish_keys(slice_raw, slice_positions).astype(jnp.bfloat16)
    slice_values = jnp.dot(slice_rows, value_weight, preferred_element_type=jnp.float32).astype(
        jnp.bfloat16
    )
    prompt_keys, prompt_values = (
        lax.all_gather(slice_keys, ("prompt", "resp"), axis=0, tiled=True),
        lax.all_gather(slice_values, ("prompt", "resp"), axis=0, tiled=True),
    )
    prompt_len = prompt_keys.shape[0]
    key_count = prompt_len + RLEN
    states = response_states[0, 0]
    positions = prompt_len + jnp.arange(RLEN, dtype=jnp.int32)
    own_raw = jnp.dot(states, key_weight, preferred_element_type=jnp.float32)
    own_keys = finish_keys(own_raw, positions).astype(jnp.bfloat16)
    own_values = jnp.dot(states, value_weight, preferred_element_type=jnp.float32).astype(
        jnp.bfloat16
    )
    keys = jnp.concatenate([prompt_keys, own_keys], axis=0)
    values = jnp.concatenate([prompt_values, own_values], axis=0)
    length = local_lengths[0]
    live = jnp.arange(RLEN, dtype=jnp.int32) < length
    coef = jnp.where(live, advantage[0] / length.astype(jnp.float32), jnp.float32(0.0))
    dout = (grad_output[0, 0].astype(jnp.float32) * coef[:, None]).astype(jnp.bfloat16)
    query = queries[0, 0]
    query_width = query.shape[1]

    def per_block(carry, block, query=query, dout=dout, keys=keys, values=values, length=length):
        acc_k, acc_v = carry
        row_start = block * QBLOCK
        query_rows = lax.dynamic_slice_in_dim(query, row_start, QBLOCK, 0)
        dout_rows = lax.dynamic_slice_in_dim(dout, row_start, QBLOCK, 0)

        def active():
            return attend(query_rows, dout_rows, keys, values, row_start, prompt_len)

        def skipped():
            return (
                jnp.zeros((QBLOCK, query_width), jnp.bfloat16),
                jnp.zeros((key_count, width), jnp.float32),
                jnp.zeros((key_count, width), jnp.float32),
            )

        grad_q, grad_k, grad_v = lax.cond(row_start < length, active, skipped)
        return ((acc_k + grad_k, acc_v + grad_v), grad_q)

    start = (jnp.zeros((key_count, width), jnp.float32), jnp.zeros((key_count, width), jnp.float32))
    (block_k, block_v), grad_blocks = lax.scan(
        per_block, start, jnp.arange(RLEN // QBLOCK, dtype=jnp.int32)
    )
    query_grads = [grad_blocks.reshape(RLEN, query_width)]
    sum_keys = block_k[:prompt_len]
    sum_values = block_v[:prompt_len]
    own_dk = keys_backward(block_k[prompt_len:], own_raw, positions).astype(jnp.bfloat16)
    own_dv = block_v[prompt_len:].astype(jnp.bfloat16)
    grad_wk = jnp.einsum("rd,rk->dk", states, own_dk, preferred_element_type=jnp.float32)
    grad_wv = jnp.einsum("rd,rk->dk", states, own_dv, preferred_element_type=jnp.float32)
    slice_dk, slice_dv = (
        lax.psum_scatter(sum_keys, ("prompt", "resp"), scatter_dimension=0, tiled=True),
        lax.psum_scatter(sum_values, ("prompt", "resp"), scatter_dimension=0, tiled=True),
    )
    slice_raw_grad = keys_backward(slice_dk, slice_raw, slice_positions).astype(jnp.bfloat16)
    grad_wk = grad_wk + jnp.einsum(
        "rd,rk->dk", slice_rows, slice_raw_grad, preferred_element_type=jnp.float32
    )
    grad_wv = grad_wv + jnp.einsum(
        "rd,rk->dk", slice_rows, slice_dv.astype(jnp.bfloat16), preferred_element_type=jnp.float32
    )
    shares = (
        lax.psum_scatter(grad_wk, ("prompt", "resp"), scatter_dimension=0, tiled=True),
        lax.psum_scatter(grad_wv, ("prompt", "resp"), scatter_dimension=0, tiled=True),
    )
    summed = lax.psum((shares[0], shares[1]), "grp")
    return (jnp.stack(query_grads, axis=0)[None], summed[0], summed[1])


def solution(mesh):
    placed = (
        P("grp", "prompt", None),
        P("grp", ("prompt", "resp"), None, None),
        P("grp", ("prompt", "resp"), None, None),
        P("grp", ("prompt", "resp"), None, None),
        P(),
        P(),
        P("grp", ("prompt", "resp")),
        P("grp", ("prompt", "resp")),
        P("grp", ("prompt", "resp")),
    )
    return jax.shard_map(
        body,
        mesh=mesh,
        in_specs=placed,
        out_specs=(
            P("grp", ("prompt", "resp"), None, None),
            P(("prompt", "resp"), None),
            P(("prompt", "resp"), None),
        ),
        check_vma=False,
    )
```

profile of v0, /device:TPU:0, one launch (start us, length us, event | category | flops | bytes accessed | tf_op | source)
XLA Modules:
  0.0 1844.8 jit_solution(5802944447283715801)
XLA Ops:
  7.3 6.4 copy.79
  13.7 5.9 fusion.25
  20.3 1.5 copy-done.5
  23.1 2.4 multiply_reduce_fusion.1
  28.2 147.1 %all_gather.7 = bf16[512,512]{1,0:T(8,128)(2,1)S(1)} all-gather(bf16[8,512]{1,0:T(8,128)(2,1)S(1)} %convolution_convert_fusion), channel_id=1, replica_groups=mesh['grp'=2,'prompt'=8,'resp'=8] {'prompt','resp'}, dimensions={0}, use_global_device_ids=true | all-gather | bytes 532480 | tf_op jit(solution)/shard_map/all_gather | solution.py:137
  176.7 4.0 copy.46
  180.6 4.0 copy.50
  184.9 150.0 %all_gather.6 = bf16[512,512]{1,0:T(8,128)(2,1)} all-gather(bf16[8,512]{1,0:T(8,128)(2,1)S(1)} %maximum_bitcast_fusion), channel_id=1, replica_groups=mesh['grp'=2,'prompt'=8,'resp'=8] {'prompt','resp'}, dimensions={0}, use_global_device_ids=true | all-gather | bytes 532480 | tf_op jit(solution)/shard_map/all_gather | solution.py:136
  336.3 2.3 pad_maximum_fusion
  338.6 2.3 copy.51
  340.8 141.7 %all-reduce = (f32[8]{0:T(128)S(1)}, f32[8]{0:T(128)S(1)}, f32[8]{0:T(128)S(1)}) all-reduce(f32[8]{0:T(128)S(1)} %get-tuple-element.262, f32[8]{0:T(128)S(1)} %fusion.46, f32[8]{0:T(128)S(1)} %get-tuple-element.261), channel_id=1, replica_groups=mesh['grp'=2,'prompt'=8,'resp'=8] {'prompt','resp'}, use_global_device_ids=true, to_apply=%region_0.0 | all-reduce | flops 24 | bytes 192 | tf_op jit(solution)/shard_map/psum | solution.py:122
  484.4 1.8 fusion.18
  486.2 61.8 %while.15 = (s32[]{:T(128)}, f32[1024,512]{0,1:T(8,128)}, f32[1024,512]{0,1:T(8,128)}, bf16[4,128,2048]{2,1,0:T(8,128)(2,1)}, s32[4]{0:T(128)S(1)}, /*index=5*/s...) while((s32[]{:T(128)}, f32[1024,512]{0,1:T(8,128)}, ...), condition=%wide.region_13.14_spmd.clone, body=%wide.region_7.13_spmd.clone.sunk | while | flops 3246392320 | bytes 116706752 | solution.py:177
  488.0 21.7 %conditional.3 = (f32[1024,512]{0,1:T(8,128)}, f32[1024,512]{0,1:T(8,128)S(1)}, bf16[1,128,2048]{1,2,0:T(8,128)(2,1)S(1)}) conditional(s32[]{:T(128)} %convert_element_type.152, () %tuple.68, (s32[]{:T(128)}, bf16[512,2048]{0,1:T(8,128)(2,1)}, bf16[1024,512]{0,1:T(8,128)(2,1)}, bf16[512,2048]{0,1:T(8,128)(2,1)}, bf16[1024,512]{0,1:T(8,128)(2,1)}) %tuple.69), branch_computations={%region_8.8_spmd, %region_9.12_spmd} | conditional | flops 3244295168 | bytes 102026464 | solution.py:173
  488.0 1.9 constant_dynamic-slice_fusion
  490.2 7.4 fusion.53
  497.5 4.1 fusion.10
  501.7 1.6 fusion.15
  504.1 1.9 fusion.2
  506.0 1.5 fusion.14
  507.6 2.1 bitcast_multiply_fusion
  509.7 4.8 select_add_fusion.3
  517.3 1.9 conditional.3
  517.6 1.6 broadcast.230
  519.2 6.0 select_add_fusion.3
  528.1 1.9 conditional.3
  528.5 1.6 broadcast.230
  530.1 6.0 select_add_fusion.3
  539.0 1.9 conditional.3
  539.3 1.6 broadcast.230
  540.9 6.0 select_add_fusion.3
  548.0 2.4 slice.48
  550.5 2.5 copy.75
  553.1 1.8 copy.54
  554.9 2.2 slice.55
  557.5 335.7 %reduce-scatter.15.cloned.1.call-done = f32[8,512]{1,0:T(8,128)} async-done(((f32[512,512]{1,0:T(8,128)}), f32[8,512]{1,0:T(8,128)}) %reduce-scatter.15.cloned.1.call-update) | async-done | bytes 16400
  896.9 5.6 bitcast_add_fusion
  902.5 9.0 copy.77
  913.5 263.1 %reduce-scatter.11.cloned.1.call-done = f32[8,512]{1,0:T(8,128)} async-done(((f32[512,512]{1,0:T(8,128)}), f32[8,512]{1,0:T(8,128)}) %reduce-scatter.11.cloned.1.call-update) | async-done | bytes 16400 | tf_op jit(solution)/shard_map/reduce_scatter | solution.py:188
  1179.8 5.6 bitcast_add_fusion.1
  1185.4 9.0 copy.73
  1194.5 294.2 %reduce-scatter.17.cloned.1.call-done = f32[64,512]{1,0:T(8,128)} async-done(((f32[4096,512]{1,0:T(8,128)}), f32[64,512]{1,0:T(8,128)}) %reduce-scatter.17.cloned.1.call-update) | async-done | bytes 131088
  1488.7 1.7 copy.78
  1490.4 309.4 %reduce-scatter.13.cloned.1.call-done = f32[64,512]{1,0:T(8,128)} async-done(((f32[4096,512]{1,0:T(8,128)}), f32[64,512]{1,0:T(8,128)}) %reduce-scatter.13.cloned.1.call-update) | async-done | bytes 131088
  1799.8 1.7 copy.74
  1801.5 33.3 %all-reduce.4.cloned.1.call-done = (f32[64,512]{0,1:T(8,128)}, f32[64,512]{0,1:T(8,128)}) async-done(((f32[64,512]{0,1:T(8,128)}, f32[64,512]{0,1:T(8,128)}), (f32[64,512]{0,1:T(8,128)}, f32[64,512]{0,1:T(8,128)})) %all-reduce.4.cloned.1.call-update) | async-done | bytes 262160 | tf_op jit(solution)/shard_map/psum | solution.py:202
  1834.9 1.7 copy.57
  1836.6 1.7 copy.58
  (132 shorter events, 24.0 us)
Async XLA Ops:
  7.2 12.5 copy-start
  7.2 886.0 %reduce-scatter.15.cloned.1.call-start = ((), (), s32[]{:S(2)}) async-start(), calls=%async_computation.6 | async-start | bytes 1064960
  13.7 5.9 copy-start.12
  19.7 2.2 copy-start.5
  19.7 3.5 copy-start.6
  23.1 161.5 %copy-start.19 = (f32[8,4,128]{2,0,1:T(8,128)}, f32[8,4,128]{2,0,1:T(8,128)S(1)}, u32[]{:S(2)}) copy-start(f32[8,4,128]{2,0,1:T(8,128)S(1)} %get-tuple-element.260) | copy-start | bytes 49156
  25.5 309.3 %copy-start.9 = (f32[512,4,128]{0,2,1:T(8,128)}, f32[512,4,128]{0,2,1:T(8,128)S(1)}, u32[]{:S(2)}) copy-start(f32[512,4,128]{0,2,1:T(8,128)S(1)} %get-tuple-element.258) | copy-start | bytes 3145732
  27.6 157.1 %copy-start.25 = (f32[8,64]{1,0:T(8,128)}, f32[8,64]{1,0:T(8,128)S(1)}, u32[]{:S(2)}) copy-start(f32[8,64]{1,0:T(8,128)S(1)} %get-tuple-element.255) | copy-start | bytes 6148
  27.6 157.1 %copy-start.27 = (f32[8,64]{1,0:T(8,128)}, f32[8,64]{1,0:T(8,128)S(1)}, u32[]{:S(2)}) copy-start(f32[8,64]{1,0:T(8,128)S(1)} %get-tuple-element.256) | copy-start | bytes 6148
  28.2 306.8 %copy-start.13 = (f32[512,64]{0,1:T(8,128)}, f32[512,64]{0,1:T(8,128)S(1)}, u32[]{:S(2)}) copy-start(f32[512,64]{0,1:T(8,128)S(1)} %get-tuple-element.253) | copy-start | bytes 393220
  28.2 306.8 %copy-start.15 = (f32[512,64]{0,1:T(8,128)}, f32[512,64]{0,1:T(8,128)S(1)}, u32[]{:S(2)}) copy-start(f32[512,64]{0,1:T(8,128)S(1)} %get-tuple-element.254) | copy-start | bytes 393220
  184.6 150.7 %copy-start.21 = (f32[512,4]{0,1:T(4,128)}, f32[512,4]{0,1:T(4,128)S(1)}, u32[]{:S(2)}) copy-start(f32[512,4]{0,1:T(4,128)S(1)} %add_rsqrt_fusion) | copy-start | bytes 24580
  184.6 150.6 %copy-start.23 = (f32[8,4]{0,1:T(4,128)}, f32[8,4]{0,1:T(4,128)S(1)}, u32[]{:S(2)}) copy-start(f32[8,4]{0,1:T(4,128)S(1)} %add_rsqrt_fusion.1) | copy-start | bytes 388
  335.0 149.4 %copy-start.11 = (bf16[1,1,512,2048]{2,3,1,0:T(8,128)(2,1)S(1)}, bf16[1,1,512,2048]{2,3,1,0:T(8,128)(2,1)}, u32[]{:S(2)}) copy-start(bf16[1,1,512,2048]{2,3,1,0:T(8,128)(2,1)} %copy.50) | copy-start | bytes 6291460
  490.0 7.6 copy-start.3
  497.5 4.2 copy-start.17
  497.5 6.5 slice-start
  501.7 2.4 slice-start.1
  504.1 1.9 copy-start.18
  506.0 1.6 copy-start.4
  548.0 5.1 copy-start.1
  553.0 623.5 %reduce-scatter.11.cloned.1.call-start = ((), (), s32[]{:S(2)}) async-start(), calls=%async_computation.4 | async-start | bytes 1064960 | tf_op jit(solution)/shard_map/reduce_scatter | solution.py:188
  557.2 931.5 %reduce-scatter.17.cloned.1.call-start = ((), (), s32[]{:S(2)}) async-start(), calls=%async_computation.7 | async-start | bytes 8519680
  894.0 1.6 copy-start.2
  894.1 2.8 copy-start.7
  911.5 0.9 copy-start.14
  911.5 1.0 copy-start.16
  911.6 1.1 copy-start.22
  911.6 265.0 %copy-start.26 = (f32[8,64]{1,0:T(8,128)S(1)}, f32[8,64]{1,0:T(8,128)}, u32[]{:S(2)}) copy-start(f32[8,64]{1,0:T(8,128)} %copy-done.25) | copy-start | bytes 6148
  911.6 265.0 %copy-start.28 = (f32[8,64]{1,0:T(8,128)S(1)}, f32[8,64]{1,0:T(8,128)}, u32[]{:S(2)}) copy-start(f32[8,64]{1,0:T(8,128)} %copy-done.27) | copy-start | bytes 6148
  911.6 265.9 %copy-start.20 = (f32[8,4,128]{2,0,1:T(8,128)S(1)}, f32[8,4,128]{2,0,1:T(8,128)}, u32[]{:S(2)}) copy-start(f32[8,4,128]{2,0,1:T(8,128)} %copy-done.19) | copy-start | bytes 49156
  911.6 265.8 %copy-start.24 = (f32[8,4]{0,1:T(4,128)S(1)}, f32[8,4]{0,1:T(4,128)}, u32[]{:S(2)}) copy-start(f32[8,4]{0,1:T(4,128)} %copy-done.23) | copy-start | bytes 388
  911.6 888.2 %reduce-scatter.13.cloned.1.call-start = ((), (), s32[]{:S(2)}) async-start(), calls=%async_computation.5 | async-start | bytes 8519680
  911.7 1.3 copy-start.10
  1177.6 2.2 copy-start.8
  1194.4 640.4 %all-reduce.4.cloned.1.call-start = ((), (), s32[]{:S(2)}) async-start(), calls=%async_computation.8 | async-start | bytes 1048576 | tf_op jit(solution)/shard_map/psum | solution.py:202
Sparse Core Ops, SparseCore 0:
  553.2 339.9 reduce-scatter.14
  895.6 280.8 reduce-scatter.10
  1179.0 309.6 reduce-scatter.16
  1490.9 308.8 reduce-scatter.12
  1802.1 32.7 all-reduce.3
where the time goes:
time: 1850 us; the launch traced here: 1840 us
  waiting for transfers between devices  1240 us (67%)
  blocking collectives  439 us (24%)
  local copies, waits for them, and re-layouts  73.1 us (4%)
  matrix products  39.2 us (2%)
  other arithmetic  35 us (2%)
    unnamed x8, waiting for transfers between devices  939 us
    reduce_scatter x1, waiting for transfers between devices, body(): lax.psum_scatter(sum_keys, ('prompt', 'resp'), scatter_dimension=0, tiled...  263 us
    all_gather x1, blocking collectives, body(): lax.all_gather(slice_keys, ('prompt', 'resp'), axis=0, tiled=True)  150 us
    all_gather x1, blocking collectives, body(): lax.all_gather(slice_values, ('prompt', 'resp'), axis=0, tiled=True)  147 us
    psum x1, blocking collectives, body(): sums = lax.psum((count, total, square), ('prompt', 'resp'))  142 us
    unnamed x62, local copies, waits for them, and re-layouts  44.9 us
  transfers between devices with their start and end apart: 5, of which 5 were waited for; matrix products, arithmetic and copies ran while one was open for 2% of the time, Pallas kernels for 0%

commit v1 on v0

v1 whole, which is shorter than its diff:
```python
import functools
import math

import jax
import jax.numpy as jnp
import numpy as np
from jax import lax
from jax.experimental import pallas as pl
from jax.experimental.pallas import tpu as pltpu
from jax.sharding import PartitionSpec as P

HEAD_DIM = 128
KVH = 4
RLEN = 512
PLEN = 512
PSH = 64
D = 4096
NADV = 8
THETA = 1000000.0
EPS = 1e-06
SCALE = 1.0 / math.sqrt(HEAD_DIM)
EXP2_SCALE = math.log2(math.e) / math.sqrt(HEAD_DIM)

F32 = jnp.float32
BF16 = jnp.bfloat16
NT = (((1,), (1,)), ((), ()))
MESH = pl.DeviceIdType.MESH


def rotary_tables():
    half = HEAD_DIM // 2
    steps = np.arange(half, dtype=np.float32)
    freq = np.power(np.float32(THETA), np.float32(-2.0) * steps / np.float32(2.0 * half))
    positions = np.arange(PLEN + RLEN, dtype=np.float32)
    angle = (positions[:, None] * freq.astype(np.float32)[None, :]).astype(np.float64)
    cosine, sine = np.cos(angle), np.sin(angle)
    return (
        np.concatenate([cosine, cosine], axis=1).astype(np.float32),
        np.concatenate([-sine, sine], axis=1).astype(np.float32),
    )


def finish_head(raw, cosine, sine):
    factor = lax.rsqrt(jnp.mean(raw * raw, axis=-1, keepdims=True) + EPS)
    normed = raw * factor
    return normed * cosine + pltpu.roll(normed, HEAD_DIM // 2, 1) * sine


def head_backward(grad, raw, cosine, sine):
    factor = lax.rsqrt(jnp.mean(raw * raw, axis=-1, keepdims=True) + EPS)
    normed = raw * factor
    unturned = grad * cosine - pltpu.roll(grad, HEAD_DIM // 2, 1) * sine
    inner = jnp.mean(unturned * normed, axis=-1, keepdims=True)
    return factor * (unturned - normed * inner)


def kernel(
    ps_h, st_h, q_h, go_h, wk_h, wv_h, rew, lens, ids, cos_t, sin_t,
    dq_h, gk_o, gv_o,
    ps_v, st_v, q_v, d_v, w_v, dq_v, x_v, xt, praw, oraw, kv, kt, dk, dv,
    g_b, pgs, pgr, sk, sv, rk1, rv1, sk2, sv2, rk2, rv2, s3, r3, st_s, st_r,
    lsem, xloc, dqsem, xs, xr, ags, agr, sts, strr, gs, gr, pss, psr,
    k1s, k1r, v1s, v1r, k2s, k2r, v2s, v2r, x3s, x3r,
):
    grp = lax.axis_index("grp")
    pr = lax.axis_index("prompt")
    rs = lax.axis_index("resp")
    y = pr // 2
    c = pr % 2
    z = rs // 2
    xlo = rs % 2
    x = grp * 2 + xlo

    def prompt_peer(k):
        return (grp, (pr + k) % 8, rs)

    def core_peer():
        return (grp, y * 2 + (1 - c), rs)

    def y_peer(k):
        return (grp, ((y + k) % 4) * 2 + c, rs)

    def z_peer(k):
        return (grp, pr, ((z + k) % 4) * 2 + xlo)

    def x_peer(k):
        other = (x + k) % 4
        return (other // 2, pr, z * 2 + other % 2)

    def pair_peer():
        return (grp, pr, z * 2 + (1 - xlo))

    def rcopy(src, dst, send, recv, dev):
        return pltpu.make_async_remote_copy(
            src_ref=src, dst_ref=dst, send_sem=send, recv_sem=recv,
            device_id=dev, device_id_type=MESH,
        )

    loads = [
        pltpu.make_async_copy(ps_h, ps_v, lsem.at[0]),
        pltpu.make_async_copy(wk_h, w_v.at[:, pl.ds(0, 512)], lsem.at[1]),
        pltpu.make_async_copy(wv_h, w_v.at[:, pl.ds(512, 512)], lsem.at[2]),
        pltpu.make_async_copy(st_h, st_v, lsem.at[3]),
        pltpu.make_async_copy(go_h, d_v, lsem.at[4]),
        pltpu.make_async_copy(q_h, q_v, lsem.at[5]),
    ]
    for load in loads:
        load.start()

    def x_local(seg):
        cols = pl.ds(pl.multiple_of(seg * 1024 + c * 512, 512), 512)
        here = pl.ds(seg * 512, 512)
        return (
            pltpu.make_async_copy(st_h.at[:, cols], x_v.at[pl.ds(0, 512), here], xloc.at[seg]),
            pltpu.make_async_copy(ps_h.at[:, cols], x_v.at[pl.ds(1024, 64), here], xloc.at[4 + seg]),
        )

    def x_remote(seg):
        cols = pl.ds(pl.multiple_of(seg * 1024 + (1 - c) * 512, 512), 512)
        here = pl.ds(seg * 512, 512)
        return (
            rcopy(st_h.at[:, cols], x_v.at[pl.ds(512, 512), here], xs.at[seg], xr.at[seg], core_peer()),
            rcopy(ps_h.at[:, cols], x_v.at[pl.ds(1088, 64), here], xs.at[4 + seg], xr.at[4 + seg], core_peer()),
        )

    barrier = pltpu.get_barrier_semaphore()
    for k in range(1, 8):
        pl.semaphore_signal(barrier, inc=1, device_id=prompt_peer(k), device_id_type=MESH)
    for k in range(1, 4):
        pl.semaphore_signal(barrier, inc=1, device_id=z_peer(k), device_id_type=MESH)
        pl.semaphore_signal(barrier, inc=1, device_id=x_peer(k), device_id_type=MESH)
    pl.semaphore_wait(barrier, 13)

    lane = lax.broadcasted_iota(jnp.int32, (8, 128), 1)
    row = lax.broadcasted_iota(jnp.int32, (8, 128), 0)
    reward = jnp.broadcast_to(rew[...], (8, 128))
    onehot = jnp.where(lane == jnp.broadcast_to(ids[...], (8, 128)), 1.0, 0.0).astype(F32)
    st_s[0] = onehot * jnp.where(
        row == 0, 1.0, jnp.where(row == 1, reward, jnp.where(row == 2, reward * reward, 0.0))
    )

    def stat_copy(slot):
        if slot < 7:
            return rcopy(st_s.at[0], st_r.at[slot], sts.at[slot], strr.at[slot], prompt_peer(slot + 1))
        if slot < 10:
            return rcopy(st_s.at[1], st_r.at[slot], sts.at[slot], strr.at[slot], z_peer(slot - 6))
        return rcopy(st_s.at[2], st_r.at[slot], sts.at[slot], strr.at[slot], pair_peer())

    for slot in range(7):
        stat_copy(slot).start()

    loads[0].wait()
    loads[1].wait()
    loads[2].wait()

    def prompt_tile(n, carry):
        cols = pl.ds(pl.multiple_of(n * 256, 256), 256)
        praw[:, cols] = jnp.dot(ps_v[...], w_v[:, cols], preferred_element_type=F32)
        return carry

    lax.fori_loop(0, 4, prompt_tile, 0)
    prow = pl.ds(pl.multiple_of(pr * PSH, PSH), PSH)
    pcos, psin = cos_t[prow, :], sin_t[prow, :]
    for h in range(KVH):
        cols = pl.ds(h * 128, 128)
        kv[prow, cols] = finish_head(praw[:, cols], pcos, psin).astype(BF16)
    kv[prow, pl.ds(512, 512)] = praw[:, pl.ds(512, 512)].astype(BF16)

    def gather(k):
        return rcopy(kv.at[prow], kv.at[prow], ags.at[k - 1], agr.at[k - 1], prompt_peer(k))

    def gathered(k):
        theirs = pl.ds(pl.multiple_of(((pr + 8 - k) % 8) * PSH, PSH), PSH)
        return rcopy(kv.at[theirs], kv.at[theirs], ags.at[k - 1], agr.at[k - 1], prompt_peer(k))

    for k in range(1, 8):
        gather(k).start()
    for seg in range(4):
        for copy in x_remote(seg):
            copy.start()

    for slot in range(7):
        stat_copy(slot).wait_recv()
    st_s[1] = st_s[0] + (
        ((st_r[0] + st_r[1]) + (st_r[2] + st_r[3])) + ((st_r[4] + st_r[5]) + st_r[6])
    )
    for slot in range(7, 10):
        stat_copy(slot).start()

    loads[3].wait()
    for seg in range(4):
        for copy in x_local(seg):
            copy.start()

    def own_tile(n, carry):
        cols = pl.ds(pl.multiple_of(n * 256, 256), 256)
        oraw[:, cols] = jnp.dot(st_v[...], w_v[:, cols], preferred_element_type=F32)
        return carry

    lax.fori_loop(0, 4, own_tile, 0)

    for slot in range(7, 10):
        stat_copy(slot).wait_recv()
    st_s[2] = (st_s[1] + st_r[7]) + (st_r[8] + st_r[9])
    stat_copy(10).start()

    own = pl.ds(PLEN, RLEN)
    ocos, osin = cos_t.at[own], sin_t.at[own]

    def own_keys(h, carry):
        cols = pl.ds(pl.multiple_of(h * 128, 128), 128)
        kv[own, cols] = finish_head(oraw[:, cols], ocos[...], osin[...]).astype(BF16)
        return carry

    lax.fori_loop(0, KVH, own_keys, 0)
    kv[own, pl.ds(512, 512)] = oraw[:, pl.ds(512, 512)].astype(BF16)

    for seg in range(4):
        for copy in x_local(seg):
            copy.wait()
        for copy in x_remote(seg):
            copy.wait_recv()

    def turn(n, carry):
        cols = pl.ds(pl.multiple_of(n * 256, 256), 256)
        xt[cols, :] = x_v[:, cols].T
        return carry

    lax.fori_loop(0, 8, turn, 0)

    stat_copy(10).wait_recv()
    sums = st_s[2] + st_r[10]
    count, total, square = sums[0:1], sums[1:2], sums[2:3]
    members = jnp.maximum(count, 1.0)
    mean = total / members
    spread = jnp.sqrt(jnp.maximum(square / members - mean * mean, 0.0))
    mine = onehot[0:1]
    own_mean = jnp.sum(mine * mean, axis=1, keepdims=True)
    own_spread = jnp.sum(mine * spread, axis=1, keepdims=True)
    advantage = (rew[...] - own_mean) / jnp.maximum(own_spread, 0.5)
    weight = advantage / lens[...].astype(F32)
    token = lax.broadcasted_iota(jnp.int32, (RLEN, 128), 0)
    live = token < jnp.broadcast_to(lens[...], (RLEN, 128))
    coef = jnp.where(live, jnp.broadcast_to(weight, (RLEN, 128)), 0.0)
    loads[4].wait()
    for n in range(16):
        cols = pl.ds(n * 128, 128)
        d_v[:, cols] = (d_v[:, cols].astype(F32) * coef).astype(BF16)
    loads[5].wait()
    for k in range(1, 8):
        gathered(k).wait_recv()

    def attend(h, b):
        count = PLEN + 128 * (b + 1)
        rows = pl.ds(b * 128, 128)
        keys = kv[pl.ds(0, count), pl.ds(pl.multiple_of(h * 128, 128), 128)]
        vals = kv[pl.ds(0, count), pl.ds(pl.multiple_of(512 + h * 128, 128), 128)]
        cols = [pl.ds(pl.multiple_of((h * 4 + j) * 128, 128), 128) for j in range(4)]
        q = jnp.concatenate([q_v[rows, cc] for cc in cols], axis=0)
        do = jnp.concatenate([d_v[rows, cc] for cc in cols], axis=0)
        s = lax.dot_general(keys, q, NT, preferred_element_type=F32)
        key = lax.broadcasted_iota(jnp.int32, (128, 512), 0)
        query = lax.broadcasted_iota(jnp.int32, (128, 512), 1) % 128
        s = jnp.concatenate(
            [s[: count - 128], jnp.where(key <= query, s[count - 128 :], -jnp.inf)], axis=0
        )
        peak = jnp.max(s, axis=0, keepdims=True)
        e = jnp.exp2((s - peak) * EXP2_SCALE)
        p = e * (1.0 / jnp.sum(e, axis=0, keepdims=True))
        dp = lax.dot_general(vals, do, NT, preferred_element_type=F32)
        delta = jnp.sum(p * dp, axis=0, keepdims=True)
        ds = (p * (dp - delta)).astype(BF16)
        gv = jnp.dot(p.astype(BF16), do, preferred_element_type=F32)
        gk = jnp.dot(ds, q, preferred_element_type=F32)
        if b == 3:
            dv[...] = gv
            dk[...] = gk
        else:
            dv[pl.ds(0, count)] += gv
            dk[pl.ds(0, count)] += gk
        dq = (jnp.dot(kt[:, pl.ds(0, count)], ds, preferred_element_type=F32) * SCALE).T.astype(BF16)
        for j, cc in enumerate(cols):
            dq_v[rows, cc] = dq[j * 128 : (j + 1) * 128]

    def g_copy(h, part):
        mine = (pl.ds(0, 512), pl.ds(1024, 64))[part]
        theirs = (pl.ds(512, 512), pl.ds(1088, 64))[part]
        return rcopy(g_b.at[h, mine], g_b.at[h, theirs], gs.at[h, part], gr.at[h, part], core_peer())

    def pg_copy(h, k):
        return rcopy(pgs.at[h, (pr + k) % 8], pgr.at[h, k - 1], pss.at[h, k - 1], psr.at[h, k - 1], prompt_peer(k))

    def k1_copy(h, k):
        return rcopy(sk.at[h, (y + k) % 4], rk1.at[h, k - 1], k1s.at[h, k - 1], k1r.at[h, k - 1], y_peer(k))

    def v1_copy(h, k):
        return rcopy(sv.at[h, (z + k) % 4], rv1.at[h, k - 1], v1s.at[h, k - 1], v1r.at[h, k - 1], z_peer(k))

    def k2_copy(h, k):
        return rcopy(sk2.at[h, (z + k) % 4], rk2.at[h, k - 1], k2s.at[h, k - 1], k2r.at[h, k - 1], z_peer(k))

    def v2_copy(h, k):
        return rcopy(sv2.at[h, (y + k) % 4], rv2.at[h, k - 1], v2s.at[h, k - 1], v2r.at[h, k - 1], y_peer(k))

    def x3_copy(h, k):
        return rcopy(s3.at[h, (x + k) % 2], r3.at[h, k - 1], x3s.at[h, k - 1], x3r.at[h, k - 1], x_peer(k))

    def dq_copy(h):
        cols = pl.ds(pl.multiple_of(h * 512, 512), 512)
        return pltpu.make_async_copy(dq_v.at[:, cols], dq_h.at[:, cols], dqsem.at[h])

    def finish(h):
        cols = pl.ds(pl.multiple_of(h * 128, 128), 128)
        for t in range(8):
            pgs[h, t, :, pl.ds(0, 128)] = (dk[pl.ds(t * 64, 64)] * SCALE).astype(BF16)
            pgs[h, t, :, pl.ds(128, 128)] = dv[pl.ds(t * 64, 64)].astype(BF16)
        for k in range(1, 8):
            pg_copy(h, k).start()
        g_b[h, pl.ds(0, 512), pl.ds(0, 128)] = head_backward(
            dk[own] * SCALE, oraw[:, cols], ocos[...], osin[...]
        ).astype(BF16)
        g_b[h, pl.ds(0, 512), pl.ds(128, 128)] = dv[own].astype(BF16)
        g_copy(h, 0).start()
        dq_copy(h).start()

    def prompt_rows(h):
        cols = pl.ds(pl.multiple_of(h * 128, 128), 128)
        total = pgs[h, pr].astype(F32)
        for k in range(1, 8):
            pg_copy(h, k).wait_recv()
            total = total + pgr[h, k - 1].astype(F32)
        g_b[h, pl.ds(1024, 64), pl.ds(0, 128)] = head_backward(
            total[:, :128], praw[:, cols], cos_t[prow, :], sin_t[prow, :]
        ).astype(BF16)
        g_b[h, pl.ds(1024, 64), pl.ds(128, 128)] = total[:, 128:].astype(BF16)
        g_copy(h, 1).start()

    def contract(h):
        g_copy(h, 0).wait_recv()
        g_copy(h, 1).wait_recv()

        def segment(seg, carry):
            out = jnp.dot(
                xt[pl.ds(pl.multiple_of(seg * 512, 512), 512), :], g_b[h], preferred_element_type=F32
            ).astype(BF16)
            sk[h, seg] = out[:, :128]
            for t in range(4):
                sv[h, t, seg] = out[t * 128 : (t + 1) * 128, 128:]
            return carry

        lax.fori_loop(0, 4, segment, 0)
        for k in range(1, 4):
            k1_copy(h, k).start()
            v1_copy(h, k).start()

    def second(h):
        for k in range(1, 4):
            k1_copy(h, k).wait_recv()
            v1_copy(h, k).wait_recv()
        total = (sk[h, y].astype(F32) + rk1[h, 0].astype(F32)) + (
            rk1[h, 1].astype(F32) + rk1[h, 2].astype(F32)
        )
        for t in range(4):
            sk2[h, t] = total[t * 128 : (t + 1) * 128].astype(BF16)
        sv2[h] = (
            (sv[h, z].astype(F32) + rv1[h, 0].astype(F32))
            + (rv1[h, 1].astype(F32) + rv1[h, 2].astype(F32))
        ).astype(BF16)
        for k in range(1, 4):
            k2_copy(h, k).start()
            v2_copy(h, k).start()

    def third(h):
        for k in range(1, 4):
            k2_copy(h, k).wait_recv()
            v2_copy(h, k).wait_recv()
        for part, (own2, got) in enumerate(((sk2[h, z], rk2), (sv2[h, y], rv2))):
            total = (own2.astype(F32) + got[h, 0].astype(F32)) + (
                got[h, 1].astype(F32) + got[h, 2].astype(F32)
            )
            s3[h, 0, :, pl.ds(part * 128, 128)] = total[:64].astype(BF16)
            s3[h, 1, :, pl.ds(part * 128, 128)] = total[64:].astype(BF16)
        for k in range(1, 4):
            x3_copy(h, k).start()

    def output(h):
        for k in range(1, 4):
            x3_copy(h, k).wait_recv()
        total = (s3[h, xlo].astype(F32) + r3[h, 0].astype(F32)) + (
            r3[h, 1].astype(F32) + r3[h, 2].astype(F32)
        )
        cols = pl.ds(pl.multiple_of(h * 128, 128), 128)
        gk_o[:, cols] = total[:, :128]
        gv_o[:, cols] = total[:, 128:]

    def head(h, carry):
        kt[...] = kv[:, pl.ds(pl.multiple_of(h * 128, 128), 128)].T
        attend(h, 3)

        @pl.when(h > 0)
        def _():
            prompt_rows(h - 1)

        @pl.when(h > 1)
        def _():
            second(h - 2)

        attend(h, 2)

        @pl.when(h > 0)
        def _():
            contract(h - 1)

        attend(h, 1)

        @pl.when(h > 1)
        def _():
            third(h - 2)

        attend(h, 0)
        finish(h)
        return carry

    lax.fori_loop(0, KVH, head, 0)
    second(2)
    prompt_rows(3)
    contract(3)
    third(2)
    second(3)
    third(3)

    def wrap(h, carry):
        output(h)
        dq_copy(h).wait()
        for part in range(2):
            g_copy(h, part).wait_send()
        for k in range(1, 8):
            pg_copy(h, k).wait_send()
        for k in range(1, 4):
            for copy in (k1_copy, v1_copy, k2_copy, v2_copy, x3_copy):
                copy(h, k).wait_send()
        return carry

    lax.fori_loop(0, KVH, wrap, 0)
    for slot in range(11):
        stat_copy(slot).wait_send()
    for k in range(1, 8):
        gather(k).wait_send()
    for seg in range(4):
        for copy in x_remote(seg):
            copy.wait_send()


def body(
    prompt_states, response_states, queries, grad_output, key_weight, value_weight,
    rewards, lengths, group_ids,
):
    cosine, sine = rotary_tables()
    hbm = pl.BlockSpec(memory_space=pl.ANY)
    vmem = pl.BlockSpec(memory_space=pltpu.VMEM)
    dma = pltpu.SemaphoreType.DMA
    scratch = [
        pltpu.VMEM((PSH, D), BF16),
        pltpu.VMEM((RLEN, D), BF16),
        pltpu.VMEM((RLEN, 2048), BF16),
        pltpu.VMEM((RLEN, 2048), BF16),
        pltpu.VMEM((D, 1024), BF16),
        pltpu.VMEM((RLEN, 2048), BF16),
        pltpu.VMEM((1152, 2048), BF16),
        pltpu.VMEM((2048, 1152), BF16),
        pltpu.VMEM((PSH, 1024), F32),
        pltpu.VMEM((RLEN, 1024), F32),
        pltpu.VMEM((1024, 1024), BF16),
        pltpu.VMEM((128, 1024), BF16),
        pltpu.VMEM((1024, 128), F32),
        pltpu.VMEM((1024, 128), F32),
        pltpu.VMEM((KVH, 1152, 256), BF16),
        pltpu.VMEM((KVH, 8, PSH, 256), BF16),
        pltpu.VMEM((KVH, 7, PSH, 256), BF16),
        pltpu.VMEM((KVH, 4, 512, 128), BF16),
        pltpu.VMEM((KVH, 4, 4, 128, 128), BF16),
        pltpu.VMEM((KVH, 3, 512, 128), BF16),
        pltpu.VMEM((KVH, 3, 4, 128, 128), BF16),
        pltpu.VMEM((KVH, 4, 128, 128), BF16),
        pltpu.VMEM((KVH, 4, 128, 128), BF16),
        pltpu.VMEM((KVH, 3, 128, 128), BF16),
        pltpu.VMEM((KVH, 3, 128, 128), BF16),
        pltpu.VMEM((KVH, 2, 64, 256), BF16),
        pltpu.VMEM((KVH, 3, 64, 256), BF16),
        pltpu.VMEM((3, 8, 128), F32),
        pltpu.VMEM((11, 8, 128), F32),
        dma((6,)), dma((8,)), dma((KVH,)), dma((8,)), dma((8,)), dma((7,)), dma((7,)),
        dma((11,)), dma((11,)), dma((KVH, 2)), dma((KVH, 2)), dma((KVH, 7)), dma((KVH, 7)),
    ] + [dma((KVH, 3)) for _ in range(10)]
    dq, gk, gv = pl.pallas_call(
        kernel,
        out_shape=(
            jax.ShapeDtypeStruct((RLEN, 2048), BF16),
            jax.ShapeDtypeStruct((64, 512), F32),
            jax.ShapeDtypeStruct((64, 512), F32),
        ),
        in_specs=[hbm] * 6 + [vmem] * 5,
        out_specs=(hbm, vmem, vmem),
        scratch_shapes=scratch,
        compiler_params=pltpu.CompilerParams(
            collective_id=0, has_side_effects=True, vmem_limit_bytes=60 * 2**20
        ),
        name="surrogate_grad",
    )(
        prompt_states[0], response_states[0, 0], queries[0, 0], grad_output[0, 0],
        key_weight, value_weight, rewards, lengths, group_ids,
        jnp.asarray(cosine), jnp.asarray(sine),
    )
    return dq[None, None], gk, gv


def solution(mesh):
    row = P("grp", ("prompt", "resp"))
    tokens = P("grp", ("prompt", "resp"), None, None)
    return jax.shard_map(
        body,
        mesh=mesh,
        in_specs=(P("grp", "prompt", None), tokens, tokens, tokens, P(), P(), row, row, row),
        out_specs=(tokens, P(("prompt", "resp"), None), P(("prompt", "resp"), None)),
        check_vma=False,
    )
```

time: 1850 us -> 113 us (0.06)
  waiting for transfers between devices: 1240 us -> 0 us
  blocking collectives: 439 us -> 0 us
  Pallas kernels: 0 us -> 106 us
  local copies, waits for them, and re-layouts: 73.1 us -> 4.52 us
  matrix products: 39.2 us -> 0 us
  other arithmetic: 35 us -> 0 us
    unnamed x8 -> x0, waiting for transfers between devices: 939 us -> none
    all_gather x2 -> x0, blocking collectives: 297 us -> none  [the longest x1 150 us: body(): lax.all_gather(slice_keys, ('prompt', 'resp'), axis=0, tiled=True)]
    reduce_scatter x1 -> x0, waiting for transfers between devices: 263 us -> none  [body(): lax.psum_scatter(sum_keys, ('prompt', 'resp'), scatter_dimension=0, tiled...]
    psum x1 -> x0, blocking collectives: 142 us -> none  [body(): sums = lax.psum((count, total, square), ('prompt', 'resp'))]
    pallas_call x0 -> x1, Pallas kernels: none -> 106 us  [body(): pl.pallas_call(kernel, out_shape=(jax.ShapeDtypeStruct((RLEN, 2048), BF16...]
    unnamed x62 -> x7, local copies, waits for them, and re-layouts: 44.9 us -> 4.52 us
    psum x1 -> x0, waiting for transfers between devices: 33.3 us -> none  [body(): summed = lax.psum((shares[0], shares[1]), 'grp')]
    dot_general x13 -> x0, matrix products: 31.9 us -> none  [the longest x1 5.92 us: body(): jnp.dot(states, value_weight, preferred_element_type=jnp.float32)]
  transfers between devices with their start and end apart: 5 -> 0, of which waited for: 5 -> 0; matrix products, arithmetic and copies ran while one was open for 2% -> 0% of each run, Pallas kernels for 0% -> 0%
where the time goes in v1:
time: 113 us
  Pallas kernels  106 us (94%)
  local copies, waits for them, and re-layouts  4.52 us (4%)
  between operations  2.6 us (2%)
    pallas_call x1, Pallas kernels, body(): pl.pallas_call(kernel, out_shape=(jax.ShapeDtypeStruct((RLEN, 2048), BF16...  106 us
    unnamed x7, local copies, waits for them, and re-layouts  4.52 us

profile of v1, /device:TPU:0, one launch (start us, length us, event | category | flops | bytes accessed | tf_op | source)
XLA Modules:
  0.0 113.1 jit_solution(10784018099486908686)
XLA Ops:
  2.6 106.0 %surrogate_grad.1 = (bf16[512,2048]{1,0:T(8,128)(2,1)}, f32[64,512]{1,0:T(8,128)}, f32[64,512]{1,0:T(8,128)}) custom-call(bf16[64,4096]{1,0:T(8,128)(2,1)} %bitcast.9, bf16[512,4096]{1,0:T(8,128)(2,1)} %bitcast.5, bf16[512,2048]{1,0:T(8,128)(2,1)} %bitcast.7, bf16[512,2048]{1,0:T(8,128)(2,1)} %bitcast.8, bf16[4096,512]{1,0:T(8,128)(2,1)} %wk_h.1, ...), custom_call_target="tpu_custom_call" | custom-call | tf_op jit(solution)/shard_map/surrogate_grad/pallas_call | solution.py:495
  108.6 0.0 copy-start.1
  108.6 0.0 copy-start
  108.6 3.2 %copy.20 = bf16[1,1,512,2048]{3,2,1,0:T(8,128)(2,1)} copy(bf16[1,1,512,2048]{3,2,1,0:T(8,128)(2,1)} %bitcast.6) | data formatting | bytes 4194304
  111.8 0.0 copy-done.1
  111.8 0.7 copy.21
  112.5 0.0 copy-done
  112.5 0.7 copy.22
Async XLA Ops:
  108.6 3.2 %copy-start.1 = (f32[64,512]{1,0:T(8,128)S(1)}, f32[64,512]{1,0:T(8,128)}, u32[]{:S(2)}) copy-start(f32[64,512]{1,0:T(8,128)} %get-tuple-element.13) | copy-start | bytes 393220
  108.6 3.9 %copy-start = (f32[64,512]{1,0:T(8,128)S(1)}, f32[64,512]{1,0:T(8,128)}, u32[]{:S(2)}) copy-start(f32[64,512]{1,0:T(8,128)} %get-tuple-element.14) | copy-start | bytes 393220

commit v2 on v1

--- a/solution.py
+++ b/solution.py
@@ -58,9 +58,10 @@
     ps_h, st_h, q_h, go_h, wk_h, wv_h, rew, lens, ids, cos_t, sin_t,
     dq_h, gk_o, gv_o,
     ps_v, st_v, q_v, d_v, w_v, dq_v, x_v, xt, praw, oraw, kv, kt, dk, dv,
-    g_b, pgs, pgr, sk, sv, rk1, rv1, sk2, sv2, rk2, rv2, s3, r3, st_s, st_r,
-    lsem, xloc, dqsem, xs, xr, ags, agr, sts, strr, gs, gr, pss, psr,
-    k1s, k1r, v1s, v1r, k2s, k2r, v2s, v2r, x3s, x3r,
+    g_b, pgs, pgr, sa, sb, sc, ra1, rb1, rc1, sa2, sb2, sc2, ra2, rb2, rc2, s3, r3, c3, rc3,
+    st_s, st_r,
+    lsem, dqsem, xs, xr, ags, agr, sts, strr, gs, gr, pss, psr, c3s, c3r,
+    a1s, a1r, b1s, b1r, c1s, c1r, a2s, a2r, b2s, b2r, c2s, c2r, x3s, x3r,
 ):
     grp = lax.axis_index("grp")
     pr = lax.axis_index("prompt")
@@ -87,6 +88,9 @@
         other = (x + k) % 4
         return (other // 2, pr, z * 2 + other % 2)
 
+    def cross_peer(k):
+        return (1 - grp, ((y + k) % 4) * 2 + c, rs)
+
     def pair_peer():
         return (grp, pr, z * 2 + (1 - xlo))
 
@@ -104,23 +108,15 @@
         pltpu.make_async_copy(go_h, d_v, lsem.at[4]),
         pltpu.make_async_copy(q_h, q_v, lsem.at[5]),
     ]
-    for load in loads:
+    for load in loads[:3]:
         load.start()
-
-    def x_local(seg):
-        cols = pl.ds(pl.multiple_of(seg * 1024 + c * 512, 512), 512)
-        here = pl.ds(seg * 512, 512)
-        return (
-            pltpu.make_async_copy(st_h.at[:, cols], x_v.at[pl.ds(0, 512), here], xloc.at[seg]),
-            pltpu.make_async_copy(ps_h.at[:, cols], x_v.at[pl.ds(1024, 64), here], xloc.at[4 + seg]),
-        )
 
     def x_remote(seg):
         cols = pl.ds(pl.multiple_of(seg * 1024 + (1 - c) * 512, 512), 512)
         here = pl.ds(seg * 512, 512)
         return (
-            rcopy(st_h.at[:, cols], x_v.at[pl.ds(512, 512), here], xs.at[seg], xr.at[seg], core_peer()),
-            rcopy(ps_h.at[:, cols], x_v.at[pl.ds(1088, 64), here], xs.at[4 + seg], xr.at[4 + seg], core_peer()),
+            rcopy(st_v.at[:, cols], x_v.at[pl.ds(0, 512), here], xs.at[seg], xr.at[seg], core_peer()),
+            rcopy(ps_v.at[:, cols], x_v.at[pl.ds(512, 64), here], xs.at[4 + seg], xr.at[4 + seg], core_peer()),
         )
 
     barrier = pltpu.get_barrier_semaphore()
@@ -129,7 +125,8 @@
     for k in range(1, 4):
         pl.semaphore_signal(barrier, inc=1, device_id=z_peer(k), device_id_type=MESH)
         pl.semaphore_signal(barrier, inc=1, device_id=x_peer(k), device_id_type=MESH)
-    pl.semaphore_wait(barrier, 13)
+        pl.semaphore_signal(barrier, inc=1, device_id=cross_peer(k), device_id_type=MESH)
+    pl.semaphore_wait(barrier, 16)
 
     lane = lax.broadcasted_iota(jnp.int32, (8, 128), 1)
     row = lax.broadcasted_iota(jnp.int32, (8, 128), 0)
@@ -152,6 +149,8 @@
     loads[0].wait()
     loads[1].wait()
     loads[2].wait()
+    for load in loads[3:]:
+        load.start()
 
     def prompt_tile(n, carry):
         cols = pl.ds(pl.multiple_of(n * 256, 256), 256)
@@ -175,9 +174,6 @@
 
     for k in range(1, 8):
         gather(k).start()
-    for seg in range(4):
-        for copy in x_remote(seg):
-            copy.start()
 
     for slot in range(7):
         stat_copy(slot).wait_recv()
@@ -189,12 +185,16 @@
 
     loads[3].wait()
     for seg in range(4):
-        for copy in x_local(seg):
+        for copy in x_remote(seg):
             copy.start()
 
     def own_tile(n, carry):
         cols = pl.ds(pl.multiple_of(n * 256, 256), 256)
         oraw[:, cols] = jnp.dot(st_v[...], w_v[:, cols], preferred_element_type=F32)
+        for t in range(2):
+            here = pl.ds(pl.multiple_of(n * 512 + t * 256, 256), 256)
+            mine = pl.ds(pl.multiple_of(n * 1024 + c * 512 + t * 256, 256), 256)
+            xt[here, pl.ds(0, 512)] = st_v[:, mine].T
         return carry
 
     lax.fori_loop(0, 4, own_tile, 0)
@@ -216,14 +216,14 @@
     kv[own, pl.ds(512, 512)] = oraw[:, pl.ds(512, 512)].astype(BF16)
 
     for seg in range(4):
-        for copy in x_local(seg):
-            copy.wait()
         for copy in x_remote(seg):
             copy.wait_recv()
 
     def turn(n, carry):
-        cols = pl.ds(pl.multiple_of(n * 256, 256), 256)
-        xt[cols, :] = x_v[:, cols].T
+        here = pl.ds(pl.multiple_of(n * 256, 256), 256)
+        mine = pl.ds(pl.multiple_of((n // 2) * 1024 + c * 512 + (n % 2) * 256, 256), 256)
+        xt[here, pl.ds(512, 512)] = x_v[pl.ds(0, 512), here].T
+        xt[here, pl.ds(1024, 128)] = jnp.concatenate([ps_v[:, mine], x_v[pl.ds(512, 64), here]], axis=0).T
         return carry
 
     lax.fori_loop(0, 8, turn, 0)
@@ -290,20 +290,31 @@
     def pg_copy(h, k):
         return rcopy(pgs.at[h, (pr + k) % 8], pgr.at[h, k - 1], pss.at[h, k - 1], psr.at[h, k - 1], prompt_peer(k))
 
-    def k1_copy(h, k):
-        return rcopy(sk.at[h, (y + k) % 4], rk1.at[h, k - 1], k1s.at[h, k - 1], k1r.at[h, k - 1], y_peer(k))
-
-    def v1_copy(h, k):
-        return rcopy(sv.at[h, (z + k) % 4], rv1.at[h, k - 1], v1s.at[h, k - 1], v1r.at[h, k - 1], z_peer(k))
-
-    def k2_copy(h, k):
-        return rcopy(sk2.at[h, (z + k) % 4], rk2.at[h, k - 1], k2s.at[h, k - 1], k2r.at[h, k - 1], z_peer(k))
-
-    def v2_copy(h, k):
-        return rcopy(sv2.at[h, (y + k) % 4], rv2.at[h, k - 1], v2s.at[h, k - 1], v2r.at[h, k - 1], y_peer(k))
+    def a1_copy(h, k):
+        return rcopy(sa.at[h, (y + k) % 4], ra1.at[h, k - 1], a1s.at[h, k - 1], a1r.at[h, k - 1], y_peer(k))
+
+    def b1_copy(h, k):
+        return rcopy(sb.at[h, (z + k) % 4], rb1.at[h, k - 1], b1s.at[h, k - 1], b1r.at[h, k - 1], z_peer(k))
+
+    def c1_copy(h, k):
+        return rcopy(sc.at[h, (x + k) % 4], rc1.at[h, k - 1], c1s.at[h, k - 1], c1r.at[h, k - 1], x_peer(k))
+
+    def a2_copy(h, k):
+        return rcopy(sa2.at[h, (z + k) % 4], ra2.at[h, k - 1], a2s.at[h, k - 1], a2r.at[h, k - 1], z_peer(k))
+
+    def b2_copy(h, k):
+        return rcopy(sb2.at[h, (y + k) % 4], rb2.at[h, k - 1], b2s.at[h, k - 1], b2r.at[h, k - 1], y_peer(k))
+
+    def c2_copy(h, k):
+        return rcopy(sc2.at[h, (z + k) % 4], rc2.at[h, k - 1], c2s.at[h, k - 1], c2r.at[h, k - 1], z_peer(k))
 
     def x3_copy(h, k):
         return rcopy(s3.at[h, (x + k) % 2], r3.at[h, k - 1], x3s.at[h, k - 1], x3r.at[h, k - 1], x_peer(k))
+
+    def c3_copy(h, slot):
+        k = slot + 1 if slot < 3 else slot - 3
+        dev = y_peer(k) if slot < 3 else cross_peer(k)
+        return rcopy(c3.at[h, (y + k) % 4], rc3.at[h, slot], c3s.at[h, slot], c3r.at[h, slot], dev)
 
     def dq_copy(h):
         cols = pl.ds(pl.multiple_of(h * 512, 512), 512)
@@ -339,59 +350,81 @@
         g_copy(h, 0).wait_recv()
         g_copy(h, 1).wait_recv()
 
-        def segment(seg, carry):
+        def segment(i, carry):
+            seg = (y + 1 + i) % 4
             out = jnp.dot(
                 xt[pl.ds(pl.multiple_of(seg * 512, 512), 512), :], g_b[h], preferred_element_type=F32
             ).astype(BF16)
-            sk[h, seg] = out[:, :128]
-            for t in range(4):
-                sv[h, t, seg] = out[t * 128 : (t + 1) * 128, 128:]
+            for zz in range(4):
+                for xx in range(2):
+                    at = zz * 128 + xx * 64
+                    sa[h, seg, zz, xx] = out[at : at + 48, :128]
+                    sb[h, zz, seg, xx] = out[at : at + 48, 128:]
+                    sc[h, xx, zz, seg] = out[at + 48 : at + 64, :128]
+                    sc[h, xx + 2, zz, seg] = out[at + 48 : at + 64, 128:]
+
+            @pl.when(i < 3)
+            def _():
+                a1_copy(h, i + 1).start()
+
             return carry
 
         lax.fori_loop(0, 4, segment, 0)
         for k in range(1, 4):
-            k1_copy(h, k).start()
-            v1_copy(h, k).start()
+            b1_copy(h, k).start()
+            c1_copy(h, k).start()
+
+    def four(own_block, got, h):
+        return (own_block.astype(F32) + got[h, 0].astype(F32)) + (
+            got[h, 1].astype(F32) + got[h, 2].astype(F32)
+        )
 
     def second(h):
         for k in range(1, 4):
-            k1_copy(h, k).wait_recv()
-            v1_copy(h, k).wait_recv()
-        total = (sk[h, y].astype(F32) + rk1[h, 0].astype(F32)) + (
-            rk1[h, 1].astype(F32) + rk1[h, 2].astype(F32)
+            c1_copy(h, k).wait_recv()
+        sc2[h] = four(sc[h, x], rc1, h).astype(BF16)
+        for k in range(1, 4):
+            c2_copy(h, k).start()
+        for k in range(1, 4):
+            a1_copy(h, k).wait_recv()
+        sa2[h] = four(sa[h, y], ra1, h).astype(BF16)
+        for k in range(1, 4):
+            a2_copy(h, k).start()
+        for k in range(1, 4):
+            b1_copy(h, k).wait_recv()
+        sb2[h] = four(sb[h, z], rb1, h).astype(BF16)
+        for k in range(1, 4):
+            b2_copy(h, k).start()
+
+    def third(h):
+        for k in range(1, 4):
+            c2_copy(h, k).wait_recv()
+        c3[h] = four(sc2[h, z], rc2, h).astype(BF16)
+        for slot in range(7):
+            c3_copy(h, slot).start()
+        for k in range(1, 4):
+            a2_copy(h, k).wait_recv()
+            b2_copy(h, k).wait_recv()
+        s3[h, :, 0] = four(sa2[h, z], ra2, h).astype(BF16)
+        s3[h, :, 1] = four(sb2[h, y], rb2, h).astype(BF16)
+        for k in range(1, 4):
+            x3_copy(h, k).start()
+
+    def output(h):
+        cols = pl.ds(pl.multiple_of(h * 128, 128), 128)
+        for slot in range(7):
+            c3_copy(h, slot).wait_recv()
+        mine = four(c3[h, y], rc3, h)
+        other = (rc3[h, 3].astype(F32) + rc3[h, 4].astype(F32)) + (
+            rc3[h, 5].astype(F32) + rc3[h, 6].astype(F32)
         )
-        for t in range(4):
-            sk2[h, t] = total[t * 128 : (t + 1) * 128].astype(BF16)
-        sv2[h] = (
-            (sv[h, z].astype(F32) + rv1[h, 0].astype(F32))
-            + (rv1[h, 1].astype(F32) + rv1[h, 2].astype(F32))
-        ).astype(BF16)
-        for k in range(1, 4):
-            k2_copy(h, k).start()
-            v2_copy(h, k).start()
-
-    def third(h):
-        for k in range(1, 4):
-            k2_copy(h, k).wait_recv()
-            v2_copy(h, k).wait_recv()
-        for part, (own2, got) in enumerate(((sk2[h, z], rk2), (sv2[h, y], rv2))):
-            total = (own2.astype(F32) + got[h, 0].astype(F32)) + (
-                got[h, 1].astype(F32) + got[h, 2].astype(F32)
-            )
-            s3[h, 0, :, pl.ds(part * 128, 128)] = total[:64].astype(BF16)
-            s3[h, 1, :, pl.ds(part * 128, 128)] = total[64:].astype(BF16)
-        for k in range(1, 4):
-            x3_copy(h, k).start()
-
-    def output(h):
+        gk_o[pl.ds(48, 16), cols] = jnp.where(grp == 0, mine, other)
+        gv_o[pl.ds(48, 16), cols] = jnp.where(grp == 0, other, mine)
         for k in range(1, 4):
             x3_copy(h, k).wait_recv()
-        total = (s3[h, xlo].astype(F32) + r3[h, 0].astype(F32)) + (
-            r3[h, 1].astype(F32) + r3[h, 2].astype(F32)
-        )
-        cols = pl.ds(pl.multiple_of(h * 128, 128), 128)
-        gk_o[:, cols] = total[:, :128]
-        gv_o[:, cols] = total[:, 128:]
+        total = four(s3[h, xlo], r3, h)
+        gk_o[pl.ds(0, 48), cols] = total[0]
+        gv_o[pl.ds(0, 48), cols] = total[1]
 
     def head(h, carry):
         kt[...] = kv[:, pl.ds(pl.multiple_of(h * 128, 128), 128)].T
@@ -420,14 +453,6 @@
         attend(h, 0)
         finish(h)
         return carry
-
-    lax.fori_loop(0, KVH, head, 0)
-    second(2)
-    prompt_rows(3)
-    contract(3)
-    third(2)
-    second(3)
-    third(3)
 
     def wrap(h, carry):
         output(h)
@@ -436,12 +461,17 @@
             g_copy(h, part).wait_send()
         for k in range(1, 8):
             pg_copy(h, k).wait_send()
-        for k in range(1, 4):
-            for copy in (k1_copy, v1_copy, k2_copy, v2_copy, x3_copy):
+            c3_copy(h, k - 1).wait_send()
+        for k in range(1, 4):
+            for copy in (a1_copy, b1_copy, c1_copy, a2_copy, b2_copy, c2_copy, x3_copy):
                 copy(h, k).wait_send()
         return carry
 
-    lax.fori_loop(0, KVH, wrap, 0)
+    lax.fori_loop(0, KVH, head, 0)
+    second(2)
+    prompt_rows(3)
+    contract(3)
+    third(2)
     for slot in range(11):
         stat_copy(slot).wait_send()
     for k in range(1, 8):
@@ -449,6 +479,10 @@
     for seg in range(4):
         for copy in x_remote(seg):
             copy.wait_send()
+    lax.fori_loop(0, 2, wrap, 0)
+    second(3)
+    third(3)
+    lax.fori_loop(2, KVH, wrap, 0)
 
 
 def body(
@@ -466,7 +500,7 @@
         pltpu.VMEM((RLEN, 2048), BF16),
         pltpu.VMEM((D, 1024), BF16),
         pltpu.VMEM((RLEN, 2048), BF16),
-        pltpu.VMEM((1152, 2048), BF16),
+        pltpu.VMEM((576, 2048), BF16),
         pltpu.VMEM((2048, 1152), BF16),
         pltpu.VMEM((PSH, 1024), F32),
         pltpu.VMEM((RLEN, 1024), F32),
@@ -477,21 +511,28 @@
         pltpu.VMEM((KVH, 1152, 256), BF16),
         pltpu.VMEM((KVH, 8, PSH, 256), BF16),
         pltpu.VMEM((KVH, 7, PSH, 256), BF16),
-        pltpu.VMEM((KVH, 4, 512, 128), BF16),
-        pltpu.VMEM((KVH, 4, 4, 128, 128), BF16),
-        pltpu.VMEM((KVH, 3, 512, 128), BF16),
-        pltpu.VMEM((KVH, 3, 4, 128, 128), BF16),
-        pltpu.VMEM((KVH, 4, 128, 128), BF16),
-        pltpu.VMEM((KVH, 4, 128, 128), BF16),
-        pltpu.VMEM((KVH, 3, 128, 128), BF16),
-        pltpu.VMEM((KVH, 3, 128, 128), BF16),
-        pltpu.VMEM((KVH, 2, 64, 256), BF16),
-        pltpu.VMEM((KVH, 3, 64, 256), BF16),
+        pltpu.VMEM((KVH, 4, 4, 2, 48, 128), BF16),
+        pltpu.VMEM((KVH, 4, 4, 2, 48, 128), BF16),
+        pltpu.VMEM((KVH, 4, 4, 4, 16, 128), BF16),
+        pltpu.VMEM((KVH, 3, 4, 2, 48, 128), BF16),
+        pltpu.VMEM((KVH, 3, 4, 2, 48, 128), BF16),
+        pltpu.VMEM((KVH, 3, 4, 4, 16, 128), BF16),
+        pltpu.VMEM((KVH, 4, 2, 48, 128), BF16),
+        pltpu.VMEM((KVH, 4, 2, 48, 128), BF16),
+        pltpu.VMEM((KVH, 4, 4, 16, 128), BF16),
+        pltpu.VMEM((KVH, 3, 2, 48, 128), BF16),
+        pltpu.VMEM((KVH, 3, 2, 48, 128), BF16),
+        pltpu.VMEM((KVH, 3, 4, 16, 128), BF16),
+        pltpu.VMEM((KVH, 2, 2, 48, 128), BF16),
+        pltpu.VMEM((KVH, 3, 2, 48, 128), BF16),
+        pltpu.VMEM((KVH, 4, 16, 128), BF16),
+        pltpu.VMEM((KVH, 7, 16, 128), BF16),
         pltpu.VMEM((3, 8, 128), F32),
         pltpu.VMEM((11, 8, 128), F32),
-        dma((6,)), dma((8,)), dma((KVH,)), dma((8,)), dma((8,)), dma((7,)), dma((7,)),
+        dma((6,)), dma((KVH,)), dma((8,)), dma((8,)), dma((7,)), dma((7,)),
         dma((11,)), dma((11,)), dma((KVH, 2)), dma((KVH, 2)), dma((KVH, 7)), dma((KVH, 7)),
-    ] + [dma((KVH, 3)) for _ in range(10)]
+        dma((KVH, 7)), dma((KVH, 7)),
+    ] + [dma((KVH, 3)) for _ in range(14)]
     dq, gk, gv = pl.pallas_call(
         kernel,
         out_shape=(

time: 113 us -> 106 us (0.938)
  Pallas kernels: 106 us -> 98.5 us
    pallas_call x1, Pallas kernels: 106 us -> 98.5 us  [body(): pl.pallas_call(kernel, out_shape=(jax.ShapeDtypeStruct((RLEN, 2048), BF16...]
where the time goes in v2:
time: 106 us
  Pallas kernels  98.5 us (93%)
  local copies, waits for them, and re-layouts  4.52 us (4%)
  between operations  2.6 us (2%)
    pallas_call x1, Pallas kernels, body(): pl.pallas_call(kernel, out_shape=(jax.ShapeDtypeStruct((RLEN, 2048), BF16...  98.5 us
    unnamed x7, local copies, waits for them, and re-layouts  4.52 us

profile of v2, /device:TPU:0, one launch (start us, length us, event | category | flops | bytes accessed | tf_op | source)
XLA Modules:
  0.0 105.6 jit_solution(909998785486226)
XLA Ops:
  2.6 98.5 %surrogate_grad.1 = (bf16[512,2048]{1,0:T(8,128)(2,1)}, f32[64,512]{1,0:T(8,128)}, f32[64,512]{1,0:T(8,128)}) custom-call(bf16[64,4096]{1,0:T(8,128)(2,1)} %bitcast.9, bf16[512,4096]{1,0:T(8,128)(2,1)} %bitcast.5, bf16[512,2048]{1,0:T(8,128)(2,1)} %bitcast.7, bf16[512,2048]{1,0:T(8,128)(2,1)} %bitcast.8, bf16[4096,512]{1,0:T(8,128)(2,1)} %wk_h.1, ...), custom_call_target="tpu_custom_call" | custom-call | tf_op jit(solution)/shard_map/surrogate_grad/pallas_call | solution.py:536
  101.1 0.0 copy-start.1
  101.1 0.0 copy-start
  101.1 3.2 %copy.20 = bf16[1,1,512,2048]{3,2,1,0:T(8,128)(2,1)} copy(bf16[1,1,512,2048]{3,2,1,0:T(8,128)(2,1)} %bitcast.6) | data formatting | bytes 4194304
  104.3 0.0 copy-done.1
  104.3 0.7 copy.21
  105.0 0.0 copy-done
  105.0 0.7 copy.22
Async XLA Ops:
  101.1 3.2 %copy-start.1 = (f32[64,512]{1,0:T(8,128)S(1)}, f32[64,512]{1,0:T(8,128)}, u32[]{:S(2)}) copy-start(f32[64,512]{1,0:T(8,128)} %get-tuple-element.13) | copy-start | bytes 393220
  101.1 3.9 %copy-start = (f32[64,512]{1,0:T(8,128)S(1)}, f32[64,512]{1,0:T(8,128)}, u32[]{:S(2)}) copy-start(f32[64,512]{1,0:T(8,128)} %get-tuple-element.14) | copy-start | bytes 393220

commit v3 on v2

--- a/solution.py
+++ b/solution.py
@@ -16,6 +16,7 @@
 PSH = 64
 D = 4096
 NADV = 8
+DBASE = 1024
 THETA = 1000000.0
 EPS = 1e-06
 SCALE = 1.0 / math.sqrt(HEAD_DIM)
@@ -55,12 +56,12 @@
 
 
 def kernel(
-    ps_h, st_h, q_h, go_h, wk_h, wv_h, rew, lens, ids, cos_t, sin_t,
-    dq_h, gk_o, gv_o,
-    ps_v, st_v, q_v, d_v, w_v, dq_v, x_v, xt, praw, oraw, kv, kt, dk, dv,
+    ps_h, st_h, q_h, go_h, wk_h, wv_h, cos_h, sin_h, rew, lens, ids,
+    dq_o, gk_o, gv_o,
+    ps_v, st_v, w_v, cos_t, sin_t, x_v, xt, praw, oraw, kv, kt, dk, dv,
     g_b, pgs, pgr, sa, sb, sc, ra1, rb1, rc1, sa2, sb2, sc2, ra2, rb2, rc2, s3, r3, c3, rc3,
     st_s, st_r,
-    lsem, dqsem, xs, xr, ags, agr, sts, strr, gs, gr, pss, psr, c3s, c3r,
+    lsem, xs, xr, ags, agr, sts, strr, gs, gr, pss, psr, c3s, c3r,
     a1s, a1r, b1s, b1r, c1s, c1r, a2s, a2r, b2s, b2r, c2s, c2r, x3s, x3r,
 ):
     grp = lax.axis_index("grp")
@@ -105,10 +106,10 @@
         pltpu.make_async_copy(wk_h, w_v.at[:, pl.ds(0, 512)], lsem.at[1]),
         pltpu.make_async_copy(wv_h, w_v.at[:, pl.ds(512, 512)], lsem.at[2]),
         pltpu.make_async_copy(st_h, st_v, lsem.at[3]),
-        pltpu.make_async_copy(go_h, d_v, lsem.at[4]),
-        pltpu.make_async_copy(q_h, q_v, lsem.at[5]),
+        pltpu.make_async_copy(cos_h, cos_t, lsem.at[4]),
+        pltpu.make_async_copy(sin_h, sin_t, lsem.at[5]),
     ]
-    for load in loads[:3]:
+    for load in loads[:3] + loads[4:6]:
         load.start()
 
     def x_remote(seg):
@@ -149,8 +150,7 @@
     loads[0].wait()
     loads[1].wait()
     loads[2].wait()
-    for load in loads[3:]:
-        load.start()
+    loads[3].start()
 
     def prompt_tile(n, carry):
         cols = pl.ds(pl.multiple_of(n * 256, 256), 256)
@@ -159,20 +159,36 @@
 
     lax.fori_loop(0, 4, prompt_tile, 0)
     prow = pl.ds(pl.multiple_of(pr * PSH, PSH), PSH)
+    loads[4].wait()
+    loads[5].wait()
     pcos, psin = cos_t[prow, :], sin_t[prow, :]
     for h in range(KVH):
         cols = pl.ds(h * 128, 128)
         kv[prow, cols] = finish_head(praw[:, cols], pcos, psin).astype(BF16)
     kv[prow, pl.ds(512, 512)] = praw[:, pl.ds(512, 512)].astype(BF16)
 
+    def shard(index):
+        return kv.at[pl.ds(pl.multiple_of(index * PSH, PSH), PSH)]
+
+    def y_shard(k, core):
+        return shard(((y + 4 - k) % 4) * 2 + core)
+
     def gather(k):
-        return rcopy(kv.at[prow], kv.at[prow], ags.at[k - 1], agr.at[k - 1], prompt_peer(k))
+        dev = core_peer() if k == 0 else y_peer(k)
+        return rcopy(shard(pr), shard(pr), ags.at[k], agr.at[k], dev)
 
     def gathered(k):
-        theirs = pl.ds(pl.multiple_of(((pr + 8 - k) % 8) * PSH, PSH), PSH)
-        return rcopy(kv.at[theirs], kv.at[theirs], ags.at[k - 1], agr.at[k - 1], prompt_peer(k))
-
-    for k in range(1, 8):
+        theirs = shard(y * 2 + (1 - c)) if k == 0 else y_shard(k, c)
+        return rcopy(theirs, theirs, ags.at[k], agr.at[k], core_peer())
+
+    def forward(k):
+        return rcopy(y_shard(k, c), y_shard(k, c), ags.at[3 + k], agr.at[3 + k], core_peer())
+
+    def forwarded(k):
+        theirs = y_shard(k, 1 - c)
+        return rcopy(theirs, theirs, ags.at[3 + k], agr.at[3 + k], core_peer())
+
+    for k in (1, 2, 3, 0):
         gather(k).start()
 
     for slot in range(7):
@@ -198,6 +214,18 @@
         return carry
 
     lax.fori_loop(0, 4, own_tile, 0)
+    late = [
+        pltpu.make_async_copy(
+            array.at[:, pl.ds(half * 1024, 1024)], w_v.at[pl.ds(base + half * 512, 512)], lsem.at[6 + n * 2 + half]
+        )
+        for n, (array, base) in enumerate(((go_h, DBASE), (q_h, 0)))
+        for half in range(2)
+    ]
+    for load in late:
+        load.start()
+    for k in range(1, 4):
+        gathered(k).wait_recv()
+        forward(k).start()
 
     for slot in range(7, 10):
         stat_copy(slot).wait_recv()
@@ -242,13 +270,17 @@
     token = lax.broadcasted_iota(jnp.int32, (RLEN, 128), 0)
     live = token < jnp.broadcast_to(lens[...], (RLEN, 128))
     coef = jnp.where(live, jnp.broadcast_to(weight, (RLEN, 128)), 0.0)
-    loads[4].wait()
-    for n in range(16):
-        cols = pl.ds(n * 128, 128)
-        d_v[:, cols] = (d_v[:, cols].astype(F32) * coef).astype(BF16)
-    loads[5].wait()
-    for k in range(1, 8):
-        gathered(k).wait_recv()
+    for half in range(2):
+        late[half].wait()
+        rows = pl.ds(DBASE + half * 512, 512)
+        for n in range(8):
+            cols = pl.ds(n * 128, 128)
+            w_v[rows, cols] = (w_v[rows, cols].astype(F32) * coef).astype(BF16)
+    late[2].wait()
+    late[3].wait()
+    gathered(0).wait_recv()
+    for k in range(1, 4):
+        forwarded(k).wait_recv()
 
     def attend(h, b):
         count = PLEN + 128 * (b + 1)
@@ -256,8 +288,12 @@
         keys = kv[pl.ds(0, count), pl.ds(pl.multiple_of(h * 128, 128), 128)]
         vals = kv[pl.ds(0, count), pl.ds(pl.multiple_of(512 + h * 128, 128), 128)]
         cols = [pl.ds(pl.multiple_of((h * 4 + j) * 128, 128), 128) for j in range(4)]
-        q = jnp.concatenate([q_v[rows, cc] for cc in cols], axis=0)
-        do = jnp.concatenate([d_v[rows, cc] for cc in cols], axis=0)
+        part = [pl.ds(pl.multiple_of((h % 2) * 512 + j * 128, 128), 128) for j in range(4)]
+        start = (h // 2) * 512 + b * 128
+        qrows = pl.ds(pl.multiple_of(start, 128), 128)
+        drows = pl.ds(pl.multiple_of(DBASE + start, 128), 128)
+        q = jnp.concatenate([w_v[qrows, cc] for cc in part], axis=0)
+        do = jnp.concatenate([w_v[drows, cc] for cc in part], axis=0)
         s = lax.dot_general(keys, q, NT, preferred_element_type=F32)
         key = lax.broadcasted_iota(jnp.int32, (128, 512), 0)
         query = lax.broadcasted_iota(jnp.int32, (128, 512), 1) % 128
@@ -280,7 +316,7 @@
             dk[pl.ds(0, count)] += gk
         dq = (jnp.dot(kt[:, pl.ds(0, count)], ds, preferred_element_type=F32) * SCALE).T.astype(BF16)
         for j, cc in enumerate(cols):
-            dq_v[rows, cc] = dq[j * 128 : (j + 1) * 128]
+            dq_o[rows, cc] = dq[j * 128 : (j + 1) * 128]
 
     def g_copy(h, part):
         mine = (pl.ds(0, 512), pl.ds(1024, 64))[part]
@@ -315,10 +351,6 @@
         k = slot + 1 if slot < 3 else slot - 3
         dev = y_peer(k) if slot < 3 else cross_peer(k)
         return rcopy(c3.at[h, (y + k) % 4], rc3.at[h, slot], c3s.at[h, slot], c3r.at[h, slot], dev)
-
-    def dq_copy(h):
-        cols = pl.ds(pl.multiple_of(h * 512, 512), 512)
-        return pltpu.make_async_copy(dq_v.at[:, cols], dq_h.at[:, cols], dqsem.at[h])
 
     def finish(h):
         cols = pl.ds(pl.multiple_of(h * 128, 128), 128)
@@ -332,7 +364,12 @@
         ).astype(BF16)
         g_b[h, pl.ds(0, 512), pl.ds(128, 128)] = dv[own].astype(BF16)
         g_copy(h, 0).start()
-        dq_copy(h).start()
+
+        @pl.when(h > 0)
+        def _():
+            for k in range(1, 4):
+                a1_copy(h - 1, k).start()
+
 
     def prompt_rows(h):
         cols = pl.ds(pl.multiple_of(h * 128, 128), 128)
@@ -346,22 +383,54 @@
         g_b[h, pl.ds(1024, 64), pl.ds(128, 128)] = total[:, 128:].astype(BF16)
         g_copy(h, 1).start()
 
+    def emit(h, seg, out):
+        out = out.astype(BF16)
+        for zz in range(4):
+            for xx in range(2):
+                at = zz * 128 + xx * 64
+                sa[h, seg, zz, xx] = out[at : at + 48, :128]
+                sb[h, zz, seg, xx] = out[at : at + 48, 128:]
+                sc[h, xx, zz, seg] = out[at + 48 : at + 64, :128]
+                sc[h, xx + 2, zz, seg] = out[at + 48 : at + 64, 128:]
+
     def contract(h):
         g_copy(h, 0).wait_recv()
         g_copy(h, 1).wait_recv()
 
-        def segment(i, carry):
+        def segment(seg, carry):
+            rows = pl.ds(pl.multiple_of(seg * 512, 512), 512)
+            emit(h, seg, jnp.dot(xt[rows, :], g_b[h], preferred_element_type=F32))
+            return carry
+
+        lax.fori_loop(0, 4, segment, 0)
+        for k in range(1, 4):
+            b1_copy(h, k).start()
+            c1_copy(h, k).start()
+
+    def contract_last(h):
+        g_copy(h, 0).wait_recv()
+
+        def responses(seg, carry):
+            rows = pl.ds(pl.multiple_of(seg * 512, 512), 512)
+            cols = pl.ds(pl.multiple_of(seg * 256, 256), 256)
+            oraw[:, cols] = jnp.dot(
+                xt[rows, pl.ds(0, 1024)], g_b[h, pl.ds(0, 1024)], preferred_element_type=F32
+            )
+            return carry
+
+        lax.fori_loop(0, 4, responses, 0)
+        prompt_rows(h)
+        second_a(h - 2)
+        g_copy(h, 1).wait_recv()
+
+        def prompts(i, carry):
             seg = (y + 1 + i) % 4
-            out = jnp.dot(
-                xt[pl.ds(pl.multiple_of(seg * 512, 512), 512), :], g_b[h], preferred_element_type=F32
-            ).astype(BF16)
-            for zz in range(4):
-                for xx in range(2):
-                    at = zz * 128 + xx * 64
-                    sa[h, seg, zz, xx] = out[at : at + 48, :128]
-                    sb[h, zz, seg, xx] = out[at : at + 48, 128:]
-                    sc[h, xx, zz, seg] = out[at + 48 : at + 64, :128]
-                    sc[h, xx + 2, zz, seg] = out[at + 48 : at + 64, 128:]
+            rows = pl.ds(pl.multiple_of(seg * 512, 512), 512)
+            cols = pl.ds(pl.multiple_of(seg * 256, 256), 256)
+            part = jnp.dot(
+                xt[rows, pl.ds(1024, 128)], g_b[h, pl.ds(1024, 128)], preferred_element_type=F32
+            )
+            emit(h, seg, oraw[:, cols] + part)
 
             @pl.when(i < 3)
             def _():
@@ -369,7 +438,7 @@
 
             return carry
 
-        lax.fori_loop(0, 4, segment, 0)
+        lax.fori_loop(0, 4, prompts, 0)
         for k in range(1, 4):
             b1_copy(h, k).start()
             c1_copy(h, k).start()
@@ -379,22 +448,24 @@
             got[h, 1].astype(F32) + got[h, 2].astype(F32)
         )
 
-    def second(h):
+    def second_bc(h):
         for k in range(1, 4):
             c1_copy(h, k).wait_recv()
         sc2[h] = four(sc[h, x], rc1, h).astype(BF16)
         for k in range(1, 4):
             c2_copy(h, k).start()
         for k in range(1, 4):
+            b1_copy(h, k).wait_recv()
+        sb2[h] = four(sb[h, z], rb1, h).astype(BF16)
+        for k in range(1, 4):
+            b2_copy(h, k).start()
+
+    def second_a(h):
+        for k in range(1, 4):
             a1_copy(h, k).wait_recv()
         sa2[h] = four(sa[h, y], ra1, h).astype(BF16)
         for k in range(1, 4):
             a2_copy(h, k).start()
-        for k in range(1, 4):
-            b1_copy(h, k).wait_recv()
-        sb2[h] = four(sb[h, z], rb1, h).astype(BF16)
-        for k in range(1, 4):
-            b2_copy(h, k).start()
 
     def third(h):
         for k in range(1, 4):
@@ -430,33 +501,36 @@
         kt[...] = kv[:, pl.ds(pl.multiple_of(h * 128, 128), 128)].T
         attend(h, 3)
 
+        @pl.when(h > 2)
+        def _():
+            second_a(h - 3)
+
+        attend(h, 2)
+        attend(h, 1)
+
         @pl.when(h > 0)
         def _():
             prompt_rows(h - 1)
 
         @pl.when(h > 1)
         def _():
-            second(h - 2)
-
-        attend(h, 2)
+            second_bc(h - 2)
+
+        attend(h, 0)
+
+        @pl.when(h > 2)
+        def _():
+            third(h - 3)
 
         @pl.when(h > 0)
         def _():
             contract(h - 1)
 
-        attend(h, 1)
-
-        @pl.when(h > 1)
-        def _():
-            third(h - 2)
-
-        attend(h, 0)
         finish(h)
         return carry
 
     def wrap(h, carry):
         output(h)
-        dq_copy(h).wait()
         for part in range(2):
             g_copy(h, part).wait_send()
         for k in range(1, 8):
@@ -468,19 +542,23 @@
         return carry
 
     lax.fori_loop(0, KVH, head, 0)
-    second(2)
-    prompt_rows(3)
-    contract(3)
-    third(2)
+    contract_last(3)
+    second_bc(2)
+    third(1)
+    second_a(2)
     for slot in range(11):
         stat_copy(slot).wait_send()
-    for k in range(1, 8):
+    for k in range(4):
         gather(k).wait_send()
+    for k in range(1, 4):
+        forward(k).wait_send()
     for seg in range(4):
         for copy in x_remote(seg):
             copy.wait_send()
     lax.fori_loop(0, 2, wrap, 0)
-    second(3)
+    third(2)
+    second_bc(3)
+    second_a(3)
     third(3)
     lax.fori_loop(2, KVH, wrap, 0)
 
@@ -490,16 +568,15 @@
     rewards, lengths, group_ids,
 ):
     cosine, sine = rotary_tables()
-    hbm = pl.BlockSpec(memory_space=pl.ANY)
+    hbm = pl.BlockSpec(memory_space=pltpu.HBM)
     vmem = pl.BlockSpec(memory_space=pltpu.VMEM)
     dma = pltpu.SemaphoreType.DMA
     scratch = [
         pltpu.VMEM((PSH, D), BF16),
         pltpu.VMEM((RLEN, D), BF16),
-        pltpu.VMEM((RLEN, 2048), BF16),
-        pltpu.VMEM((RLEN, 2048), BF16),
         pltpu.VMEM((D, 1024), BF16),
-        pltpu.VMEM((RLEN, 2048), BF16),
+        pltpu.VMEM((PLEN + RLEN, 128), F32),
+        pltpu.VMEM((PLEN + RLEN, 128), F32),
         pltpu.VMEM((576, 2048), BF16),
         pltpu.VMEM((2048, 1152), BF16),
         pltpu.VMEM((PSH, 1024), F32),
@@ -529,7 +606,7 @@
         pltpu.VMEM((KVH, 7, 16, 128), BF16),
         pltpu.VMEM((3, 8, 128), F32),
         pltpu.VMEM((11, 8, 128), F32),
-        dma((6,)), dma((KVH,)), dma((8,)), dma((8,)), dma((7,)), dma((7,)),
+        dma((10,)), dma((8,)), dma((8,)), dma((7,)), dma((7,)),
         dma((11,)), dma((11,)), dma((KVH, 2)), dma((KVH, 2)), dma((KVH, 7)), dma((KVH, 7)),
         dma((KVH, 7)), dma((KVH, 7)),
     ] + [dma((KVH, 3)) for _ in range(14)]
@@ -540,17 +617,17 @@
             jax.ShapeDtypeStruct((64, 512), F32),
             jax.ShapeDtypeStruct((64, 512), F32),
         ),
-        in_specs=[hbm] * 6 + [vmem] * 5,
-        out_specs=(hbm, vmem, vmem),
+        in_specs=[hbm] * 8 + [vmem] * 3,
+        out_specs=(vmem, vmem, vmem),
         scratch_shapes=scratch,
         compiler_params=pltpu.CompilerParams(
-            collective_id=0, has_side_effects=True, vmem_limit_bytes=60 * 2**20
+            collective_id=0, has_side_effects=True, vmem_limit_bytes=51 * 2**20
         ),
         name="surrogate_grad",
     )(
-        prompt_states[0], response_states[0, 0], queries[0, 0], grad_output[0, 0],
-        key_weight, value_weight, rewards, lengths, group_ids,
-        jnp.asarray(cosine), jnp.asarray(sine),
+        *[pltpu.with_memory_space_constraint(a, pltpu.HBM) for a in (prompt_states[0], response_states[0, 0], queries[0, 0], grad_output[0, 0])],
+        key_weight, value_weight, *[pltpu.with_memory_space_constraint(jnp.asarray(a), pltpu.HBM) for a in (cosine, sine)],
+        rewards, lengths, group_ids,
     )
     return dq[None, None], gk, gv
 

time: 106 us -> 94 us (0.89)
  Pallas kernels: 98.5 us -> 88.6 us
  local copies, waits for them, and re-layouts: 4.52 us -> 2.63 us
    pallas_call x1, Pallas kernels: 98.5 us -> 88.6 us  [body(): pl.pallas_call(kernel, out_shape=(jax.ShapeDtypeStruct((RLEN, 2048), BF16...]
    unnamed x7 -> x3, local copies, waits for them, and re-layouts: 4.52 us -> 2.63 us
where the time goes in v3:
time: 94 us; the launch traced here: 93.8 us
  Pallas kernels  88.6 us (94%)
  local copies, waits for them, and re-layouts  2.63 us (3%)
  between operations  2.58 us (3%)
    pallas_call x1, Pallas kernels, body(): pl.pallas_call(kernel, out_shape=(jax.ShapeDtypeStruct((RLEN, 2048), BF16...  88.6 us
    unnamed x3, local copies, waits for them, and re-layouts  2.63 us

profile of v3, /device:TPU:0, one launch (start us, length us, event | category | flops | bytes accessed | tf_op | source)
XLA Modules:
  0.0 93.8 jit_solution(3932073191123263494)
XLA Ops:
  2.6 88.6 %surrogate_grad.1 = (bf16[512,2048]{1,0:T(8,128)(2,1)S(1)}, f32[64,512]{1,0:T(8,128)S(1)}, f32[64,512]{1,0:T(8,128)S(1)}) custom-call(bf16[64,4096]{1,0:T(8,128)(2,1)} %bitcast.9, bf16[512,4096]{1,0:T(8,128)(2,1)} %bitcast.6, bf16[512,2048]{1,0:T(8,128)(2,1)} %bitcast.7, bf16[512,2048]{1,0:T(8,128)(2,1)} %bitcast.8, bf16[4096,512]{1,0:T(8,128)(2,1)} %wk_h.1, ...), custom_call_target="tpu_custom_call" | custom-call | tf_op jit(solution)/shard_map/surrogate_grad/pallas_call | solution.py:613
  91.2 1.3 %copy.20 = bf16[1,1,512,2048]{3,2,1,0:T(8,128)(2,1)} copy(bf16[1,1,512,2048]{3,2,1,0:T(8,128)(2,1)S(1)} %bitcast.5) | data formatting | bytes 4194304
  92.5 0.7 copy.21
  93.2 0.7 copy.22

commit v4 on v3

--- a/solution.py
+++ b/solution.py
@@ -149,7 +149,6 @@
 
     loads[0].wait()
     loads[1].wait()
-    loads[2].wait()
     loads[3].start()
 
     def prompt_tile(n, carry):
@@ -157,7 +156,9 @@
         praw[:, cols] = jnp.dot(ps_v[...], w_v[:, cols], preferred_element_type=F32)
         return carry
 
-    lax.fori_loop(0, 4, prompt_tile, 0)
+    lax.fori_loop(0, 2, prompt_tile, 0)
+    loads[2].wait()
+    lax.fori_loop(2, 4, prompt_tile, 0)
     prow = pl.ds(pl.multiple_of(pr * PSH, PSH), PSH)
     loads[4].wait()
     loads[5].wait()
@@ -302,9 +303,10 @@
         )
         peak = jnp.max(s, axis=0, keepdims=True)
         e = jnp.exp2((s - peak) * EXP2_SCALE)
-        p = e * (1.0 / jnp.sum(e, axis=0, keepdims=True))
+        inverse = 1.0 / jnp.sum(e, axis=0, keepdims=True)
         dp = lax.dot_general(vals, do, NT, preferred_element_type=F32)
-        delta = jnp.sum(p * dp, axis=0, keepdims=True)
+        delta = jnp.sum(e * dp, axis=0, keepdims=True) * inverse
+        p = e * inverse
         ds = (p * (dp - delta)).astype(BF16)
         gv = jnp.dot(p.astype(BF16), do, preferred_element_type=F32)
         gk = jnp.dot(ds, q, preferred_element_type=F32)
@@ -419,8 +421,9 @@
             return carry
 
         lax.fori_loop(0, 4, responses, 0)
+        second_a(h - 2)
         prompt_rows(h)
-        second_a(h - 2)
+        second_bc(h - 1)
         g_copy(h, 1).wait_recv()
 
         def prompts(i, carry):
@@ -543,7 +546,6 @@
 
     lax.fori_loop(0, KVH, head, 0)
     contract_last(3)
-    second_bc(2)
     third(1)
     second_a(2)
     for slot in range(11):
@@ -555,10 +557,11 @@
     for seg in range(4):
         for copy in x_remote(seg):
             copy.wait_send()
-    lax.fori_loop(0, 2, wrap, 0)
-    third(2)
+    lax.fori_loop(0, 1, wrap, 0)
     second_bc(3)
     second_a(3)
+    third(2)
+    lax.fori_loop(1, 2, wrap, 0)
     third(3)
     lax.fori_loop(2, KVH, wrap, 0)
 

time: 94 us -> 91.6 us (0.974)
  Pallas kernels: 88.6 us -> 86.3 us
    pallas_call x1, Pallas kernels: 88.6 us -> 86.3 us  [body(): pl.pallas_call(kernel, out_shape=(jax.ShapeDtypeStruct((RLEN, 2048), BF16...]
where the time goes in v4:
time: 91.6 us; the launch traced here: 91.5 us
  Pallas kernels  86.3 us (94%)
  local copies, waits for them, and re-layouts  2.63 us (3%)
  between operations  2.58 us (3%)
    pallas_call x1, Pallas kernels, body(): pl.pallas_call(kernel, out_shape=(jax.ShapeDtypeStruct((RLEN, 2048), BF16...  86.3 us
    unnamed x3, local copies, waits for them, and re-layouts  2.63 us

profile of v4, /device:TPU:0, one launch (start us, length us, event | category | flops | bytes accessed | tf_op | source)
XLA Modules:
  0.0 91.5 jit_solution(13585905826852920794)
XLA Ops:
  2.6 86.3 %surrogate_grad.1 = (bf16[512,2048]{1,0:T(8,128)(2,1)S(1)}, f32[64,512]{1,0:T(8,128)S(1)}, f32[64,512]{1,0:T(8,128)S(1)}) custom-call(bf16[64,4096]{1,0:T(8,128)(2,1)} %bitcast.9, bf16[512,4096]{1,0:T(8,128)(2,1)} %bitcast.6, bf16[512,2048]{1,0:T(8,128)(2,1)} %bitcast.7, bf16[512,2048]{1,0:T(8,128)(2,1)} %bitcast.8, bf16[4096,512]{1,0:T(8,128)(2,1)} %wk_h.1, ...), custom_call_target="tpu_custom_call" | custom-call | tf_op jit(solution)/shard_map/surrogate_grad/pallas_call | solution.py:616
  88.9 1.3 %copy.20 = bf16[1,1,512,2048]{3,2,1,0:T(8,128)(2,1)} copy(bf16[1,1,512,2048]{3,2,1,0:T(8,128)(2,1)S(1)} %bitcast.5) | data formatting | bytes 4194304
  90.2 0.7 copy.21
  90.9 0.7 copy.22

commit v5 on v4

--- a/solution.py
+++ b/solution.py
@@ -359,7 +359,7 @@
         for t in range(8):
             pgs[h, t, :, pl.ds(0, 128)] = (dk[pl.ds(t * 64, 64)] * SCALE).astype(BF16)
             pgs[h, t, :, pl.ds(128, 128)] = dv[pl.ds(t * 64, 64)].astype(BF16)
-        for k in range(1, 8):
+        for k in (4, 3, 5, 2, 6, 1, 7):
             pg_copy(h, k).start()
         g_b[h, pl.ds(0, 512), pl.ds(0, 128)] = head_backward(
             dk[own] * SCALE, oraw[:, cols], ocos[...], osin[...]
@@ -405,7 +405,7 @@
             return carry
 
         lax.fori_loop(0, 4, segment, 0)
-        for k in range(1, 4):
+        for k in (2, 1, 3):
             b1_copy(h, k).start()
             c1_copy(h, k).start()
 
@@ -427,7 +427,7 @@
         g_copy(h, 1).wait_recv()
 
         def prompts(i, carry):
-            seg = (y + 1 + i) % 4
+            seg = (y + 2 + i) % 4
             rows = pl.ds(pl.multiple_of(seg * 512, 512), 512)
             cols = pl.ds(pl.multiple_of(seg * 256, 256), 256)
             part = jnp.dot(
@@ -435,14 +435,14 @@
             )
             emit(h, seg, oraw[:, cols] + part)
 
-            @pl.when(i < 3)
+            @pl.when(i != 2)
             def _():
-                a1_copy(h, i + 1).start()
+                a1_copy(h, (2 + i) % 4).start()
 
             return carry
 
         lax.fori_loop(0, 4, prompts, 0)
-        for k in range(1, 4):
+        for k in (2, 1, 3):
             b1_copy(h, k).start()
             c1_copy(h, k).start()
 
@@ -455,33 +455,33 @@
         for k in range(1, 4):
             c1_copy(h, k).wait_recv()
         sc2[h] = four(sc[h, x], rc1, h).astype(BF16)
-        for k in range(1, 4):
+        for k in (2, 1, 3):
             c2_copy(h, k).start()
         for k in range(1, 4):
             b1_copy(h, k).wait_recv()
         sb2[h] = four(sb[h, z], rb1, h).astype(BF16)
-        for k in range(1, 4):
+        for k in (2, 1, 3):
             b2_copy(h, k).start()
 
     def second_a(h):
         for k in range(1, 4):
             a1_copy(h, k).wait_recv()
         sa2[h] = four(sa[h, y], ra1, h).astype(BF16)
-        for k in range(1, 4):
+        for k in (2, 1, 3):
             a2_copy(h, k).start()
 
     def third(h):
         for k in range(1, 4):
             c2_copy(h, k).wait_recv()
         c3[h] = four(sc2[h, z], rc2, h).astype(BF16)
-        for slot in range(7):
+        for slot in (5, 4, 6, 1, 3, 0, 2):
             c3_copy(h, slot).start()
         for k in range(1, 4):
             a2_copy(h, k).wait_recv()
             b2_copy(h, k).wait_recv()
         s3[h, :, 0] = four(sa2[h, z], ra2, h).astype(BF16)
         s3[h, :, 1] = four(sb2[h, y], rb2, h).astype(BF16)
-        for k in range(1, 4):
+        for k in (2, 1, 3):
             x3_copy(h, k).start()
 
     def output(h):

time: 91.6 us -> 90.1 us (0.984)
  Pallas kernels: 86.3 us -> 84.8 us
    pallas_call x1, Pallas kernels: 86.3 us -> 84.8 us  [body(): pl.pallas_call(kernel, out_shape=(jax.ShapeDtypeStruct((RLEN, 2048), BF16...]
where the time goes in v5:
time: 90.1 us; the launch traced here: 90 us
  Pallas kernels  84.8 us (94%)
  local copies, waits for them, and re-layouts  2.63 us (3%)
  between operations  2.58 us (3%)
    pallas_call x1, Pallas kernels, body(): pl.pallas_call(kernel, out_shape=(jax.ShapeDtypeStruct((RLEN, 2048), BF16...  84.8 us
    unnamed x3, local copies, waits for them, and re-layouts  2.63 us

profile of v5, /device:TPU:0, one launch (start us, length us, event | category | flops | bytes accessed | tf_op | source)
XLA Modules:
  0.0 90.0 jit_solution(7491398173152535117)
XLA Ops:
  2.6 84.8 %surrogate_grad.1 = (bf16[512,2048]{1,0:T(8,128)(2,1)S(1)}, f32[64,512]{1,0:T(8,128)S(1)}, f32[64,512]{1,0:T(8,128)S(1)}) custom-call(bf16[64,4096]{1,0:T(8,128)(2,1)} %bitcast.9, bf16[512,4096]{1,0:T(8,128)(2,1)} %bitcast.6, bf16[512,2048]{1,0:T(8,128)(2,1)} %bitcast.7, bf16[512,2048]{1,0:T(8,128)(2,1)} %bitcast.8, bf16[4096,512]{1,0:T(8,128)(2,1)} %wk_h.1, ...), custom_call_target="tpu_custom_call" | custom-call | tf_op jit(solution)/shard_map/surrogate_grad/pallas_call | solution.py:616
  87.3 1.3 %copy.20 = bf16[1,1,512,2048]{3,2,1,0:T(8,128)(2,1)} copy(bf16[1,1,512,2048]{3,2,1,0:T(8,128)(2,1)S(1)} %bitcast.5) | data formatting | bytes 4194304
  88.7 0.7 copy.21
  89.3 0.7 copy.22

commit v6 on v5

--- a/solution.py
+++ b/solution.py
@@ -189,7 +189,7 @@
         theirs = y_shard(k, 1 - c)
         return rcopy(theirs, theirs, ags.at[3 + k], agr.at[3 + k], core_peer())
 
-    for k in (1, 2, 3, 0):
+    for k in (2, 1, 3, 0):
         gather(k).start()
 
     for slot in range(7):
@@ -224,7 +224,7 @@
     ]
     for load in late:
         load.start()
-    for k in range(1, 4):
+    for k in (1, 3, 2):
         gathered(k).wait_recv()
         forward(k).start()
 

time: 90.1 us -> 90 us (level)
  no operation moved by 1% of the time
where the time goes in v6:
time: 90 us; the launch traced here: 89.8 us
  Pallas kernels  84.6 us (94%)
  local copies, waits for them, and re-layouts  2.63 us (3%)
  between operations  2.58 us (3%)
    pallas_call x1, Pallas kernels, body(): pl.pallas_call(kernel, out_shape=(jax.ShapeDtypeStruct((RLEN, 2048), BF16...  84.6 us
    unnamed x3, local copies, waits for them, and re-layouts  2.63 us

profile of v6, /device:TPU:0, one launch (start us, length us, event | category | flops | bytes accessed | tf_op | source)
XLA Modules:
  0.0 89.8 jit_solution(8780982221432139393)
XLA Ops:
  2.6 84.6 %surrogate_grad.1 = (bf16[512,2048]{1,0:T(8,128)(2,1)S(1)}, f32[64,512]{1,0:T(8,128)S(1)}, f32[64,512]{1,0:T(8,128)S(1)}) custom-call(bf16[64,4096]{1,0:T(8,128)(2,1)} %bitcast.9, bf16[512,4096]{1,0:T(8,128)(2,1)} %bitcast.6, bf16[512,2048]{1,0:T(8,128)(2,1)} %bitcast.7, bf16[512,2048]{1,0:T(8,128)(2,1)} %bitcast.8, bf16[4096,512]{1,0:T(8,128)(2,1)} %wk_h.1, ...), custom_call_target="tpu_custom_call" | custom-call | tf_op jit(solution)/shard_map/surrogate_grad/pallas_call | solution.py:616
  87.2 1.3 %copy.20 = bf16[1,1,512,2048]{3,2,1,0:T(8,128)(2,1)} copy(bf16[1,1,512,2048]{3,2,1,0:T(8,128)(2,1)S(1)} %bitcast.5) | data formatting | bytes 4194304
  88.5 0.7 copy.21
  89.2 0.7 copy.22

commit v7 on v5

--- a/solution.py
+++ b/solution.py
@@ -427,7 +427,8 @@
         g_copy(h, 1).wait_recv()
 
         def prompts(i, carry):
-            seg = (y + 2 + i) % 4
+            k = (2 + i) * (1 - i // 2) + (3 - i) * (i // 2)
+            seg = (y + k) % 4
             rows = pl.ds(pl.multiple_of(seg * 512, 512), 512)
             cols = pl.ds(pl.multiple_of(seg * 256, 256), 256)
             part = jnp.dot(
@@ -435,9 +436,9 @@
             )
             emit(h, seg, oraw[:, cols] + part)
 
-            @pl.when(i != 2)
+            @pl.when(i < 3)
             def _():
-                a1_copy(h, (2 + i) % 4).start()
+                a1_copy(h, k).start()
 
             return carry
 

time: 90.1 us -> 90.1 us (level)
  no operation moved by 1% of the time
where the time goes in v7:
time: 90.1 us; the launch traced here: 90 us
  Pallas kernels  84.8 us (94%)
  local copies, waits for them, and re-layouts  2.63 us (3%)
  between operations  2.58 us (3%)
    pallas_call x1, Pallas kernels, body(): pl.pallas_call(kernel, out_shape=(jax.ShapeDtypeStruct((RLEN, 2048), BF16...  84.8 us
    unnamed x3, local copies, waits for them, and re-layouts  2.63 us

profile of v7, /device:TPU:0, one launch (start us, length us, event | category | flops | bytes accessed | tf_op | source)
XLA Modules:
  0.0 90.0 jit_solution(12672894612139540577)
XLA Ops:
  2.6 84.8 %surrogate_grad.1 = (bf16[512,2048]{1,0:T(8,128)(2,1)S(1)}, f32[64,512]{1,0:T(8,128)S(1)}, f32[64,512]{1,0:T(8,128)S(1)}) custom-call(bf16[64,4096]{1,0:T(8,128)(2,1)} %bitcast.9, bf16[512,4096]{1,0:T(8,128)(2,1)} %bitcast.6, bf16[512,2048]{1,0:T(8,128)(2,1)} %bitcast.7, bf16[512,2048]{1,0:T(8,128)(2,1)} %bitcast.8, bf16[4096,512]{1,0:T(8,128)(2,1)} %wk_h.1, ...), custom_call_target="tpu_custom_call" | custom-call | tf_op jit(solution)/shard_map/surrogate_grad/pallas_call | solution.py:617
  87.3 1.3 %copy.20 = bf16[1,1,512,2048]{3,2,1,0:T(8,128)(2,1)} copy(bf16[1,1,512,2048]{3,2,1,0:T(8,128)(2,1)S(1)} %bitcast.5) | data formatting | bytes 4194304
  88.7 0.7 copy.21
  89.3 0.7 copy.22
